TPU v7x, 32 devices: a whole 2x2x4 slice. The times are simulated.
32 devices in a mesh: dp: 16 (over z, y, core), tensor: 2 (over x).
Axes of the slice: x: 2, y: 2, z: 4, core: 2. Of those that a mesh axis runs over, the one named last changes fastest.
Arguments:
- tokens: bfloat16 [16384, 1024], P(('dp', 'tensor')), may hold values from -6 to 6
- gain_one: float32 [1024], P(('dp', 'tensor')), may hold values from 0.5 to 1.5
- shift_one: float32 [1024], P(('dp', 'tensor')), may hold values from -2 to 2
- w_qkv: bfloat16 [3, 1024, 1024], P(None, 'dp', 'tensor'), may hold values from -0.1875 to 0.1875
- bias_qv: bfloat16 [2, 16, 64], P(None, 'tensor', 'dp'), may hold values from -2 to 2
- w_out: bfloat16 [1024, 1024], P('tensor', 'dp'), may hold values from -0.5 to 0.5
- bias_out: float32 [1024], P(('dp', 'tensor')), may hold values from -2 to 2
- gain_two: float32 [1024], P(('dp', 'tensor')), may hold values from 0.5 to 1.5
- shift_two: float32 [1024], P(('dp', 'tensor')), may hold values from -2 to 2
- w_up: bfloat16 [1024, 4096], P('dp', 'tensor'), may hold values from -0.1875 to 0.1875
- bias_up: bfloat16 [32, 128], P('tensor', 'dp'), may hold values from -2 to 2
- w_down: bfloat16 [4096, 1024], P('tensor', 'dp'), may hold values from -0.09375 to 0.09375
- bias_down: float32 [1024], P(('dp', 'tensor')), may hold values from -2 to 2
- cotangent: bfloat16 [16384, 1024], P(('dp', 'tensor')), may hold values from -6 to 6
Outputs:
- mixed: bfloat16 [16384, 1024], P(('dp', 'tensor'))
- grad_tokens: bfloat16 [16384, 1024], P(('dp', 'tensor'))
- grad_gain_one: float32 [1024], P(('dp', 'tensor'))
- grad_shift_one: float32 [1024], P(('dp', 'tensor'))
- grad_qkv: float32 [3, 1024, 1024], P(None, 'dp', 'tensor')
- grad_bias_qv: float32 [2, 16, 64], P(None, 'tensor', 'dp')
- grad_out: float32 [1024, 1024], P('tensor', 'dp')
- grad_bias_out: float32 [1024], P(('dp', 'tensor'))
- grad_gain_two: float32 [1024], P(('dp', 'tensor'))
- grad_shift_two: float32 [1024], P(('dp', 'tensor'))
- grad_up: float32 [1024, 4096], P('dp', 'tensor')
- grad_bias_up: float32 [32, 128], P('tensor', 'dp')
- grad_down: float32 [4096, 1024], P('tensor', 'dp')
- grad_bias_down: float32 [1024], P(('dp', 'tensor'))
All inputs are finite; a program needn't handle non-finite values.
Results may differ from a plain program's by a relative error of at most 0.019.
Values may be sent and summed in bfloat16 or wider, within the bound.
A program may use at most 192 MiB of HBM per device.

v0:
```python
import math

import jax
import jax.numpy as jnp
from jax import lax
from jax.sharding import PartitionSpec as P

H = 16
HD = 64
SEQ_LEN = 1024


EPSILON = 1e-05
MASKED = -1e30


def normalize(values):
    centred = values - jnp.mean(values, axis=-1, keepdims=True)
    inverse = lax.rsqrt(jnp.mean(centred * centred, axis=-1, keepdims=True) + EPSILON)
    return (centred * inverse, inverse)


def norm_backward(grad, normed, inverse, gain):
    scaled = grad * gain
    return inverse * (
        scaled
        - jnp.mean(scaled, axis=-1, keepdims=True)
        - normed * jnp.mean(scaled * normed, axis=-1, keepdims=True)
    )


def smooth_gate(values):
    return jax.nn.gelu(values, approximate=True)


def block_scores(query, keys, slopes, q_start, scale):
    products = jnp.einsum("sqhd,skhd->shqk", query, keys, preferred_element_type=jnp.float32)
    q_pos = q_start + lax.iota(jnp.int32, query.shape[1])
    k_pos = lax.iota(jnp.int32, keys.shape[1])
    offset = (k_pos[None, :] - q_pos[:, None]).astype(jnp.float32)
    scores = products * scale + slopes[None, :, None, None] * offset[None, None]
    return jnp.where((offset <= 0.0)[None, None], scores, MASKED)


def local(
    tokens,
    gain_one,
    shift_one,
    w_qkv,
    bias_qv,
    w_out,
    bias_out,
    gain_two,
    shift_two,
    w_up,
    bias_up,
    w_down,
    bias_down,
    cotangent,
):
    gain_a, shift_a, out_shift, gain_b, shift_b, down_shift = (
        lax.all_gather(gain_one, ("dp", "tensor"), axis=0, tiled=True),
        lax.all_gather(shift_one, ("dp", "tensor"), axis=0, tiled=True),
        lax.all_gather(bias_out, ("dp", "tensor"), axis=0, tiled=True),
        lax.all_gather(gain_two, ("dp", "tensor"), axis=0, tiled=True),
        lax.all_gather(shift_two, ("dp", "tensor"), axis=0, tiled=True),
        lax.all_gather(bias_down, ("dp", "tensor"), axis=0, tiled=True),
    )
    qkv_full, qv_shift, out_full, up_full, up_shift, down_full = (
        lax.all_gather(w_qkv, "dp", axis=1, tiled=True),
        lax.all_gather(bias_qv, "dp", axis=2, tiled=True),
        lax.all_gather(w_out, "dp", axis=1, tiled=True),
        lax.all_gather(w_up, "dp", axis=0, tiled=True),
        lax.all_gather(bias_up, "dp", axis=1, tiled=True),
        lax.all_gather(w_down, "dp", axis=1, tiled=True),
    )
    parts = lax.axis_size("tensor")
    rows = tokens.shape[0]
    group = rows * parts
    length = min(SEQ_LEN, group)
    sequences = group // length
    qblock = min(512, length)
    starts = list(range(0, length, qblock))
    local_heads = qkv_full.shape[2] // HD
    width = local_heads * HD
    scale = 1.0 / math.sqrt(HD)
    head_ids = lax.axis_index("tensor") * local_heads + lax.iota(jnp.int32, local_heads)
    slopes = jnp.exp2(-8.0 * (head_ids + 1).astype(jnp.float32) / H)
    inputs = tokens.astype(jnp.float32)
    normed_one, inverse_one = normalize(inputs)
    low_one = (normed_one * gain_a + shift_a).astype(jnp.bfloat16)
    full_one = lax.all_gather(low_one, "tensor", axis=0, tiled=True)
    qkv_shift = jnp.stack(
        [qv_shift[0].reshape(width), jnp.zeros((width,), jnp.bfloat16), qv_shift[1].reshape(width)]
    ).astype(jnp.float32)
    projected = jnp.einsum("rd,cde->cre", full_one, qkv_full, preferred_element_type=jnp.float32)
    qkv_low = (projected + qkv_shift[:, None, :]).astype(jnp.bfloat16)

    def split_heads(matrix):
        return matrix.reshape(sequences, length, local_heads, HD)

    query = split_heads(qkv_low[0])
    keys = split_heads(qkv_low[1])
    values = split_heads(qkv_low[2])
    outputs = []
    log_sums = []
    for q_start in starts:
        q_end = q_start + qblock
        scores = block_scores(query[:, q_start:q_end], keys[:, :q_end], slopes, q_start, scale)
        row_max = jnp.max(scores, axis=-1, keepdims=True)
        exponent = jnp.exp(scores - row_max)
        row_total = jnp.sum(exponent, axis=-1, keepdims=True)
        probs = (exponent / row_total).astype(jnp.bfloat16)
        outputs.append(
            jnp.einsum(
                "shqk,skhd->sqhd", probs, values[:, :q_end], preferred_element_type=jnp.float32
            )
        )
        log_sums.append(row_max + jnp.log(row_total))
    attended = jnp.concatenate(outputs, axis=1).reshape(group, width).astype(jnp.bfloat16)
    piece = attended
    middle = (
        inputs
        + lax.psum_scatter(
            jnp.dot(piece, out_full, preferred_element_type=jnp.float32).astype(jnp.bfloat16),
            "tensor",
            scatter_dimension=0,
            tiled=True,
        ).astype(jnp.float32)
        + out_shift
    )
    normed_two, inverse_two = normalize(middle)
    low_two = (normed_two * gain_b + shift_b).astype(jnp.bfloat16)
    full_two = lax.all_gather(low_two, "tensor", axis=0, tiled=True)
    hidden = jnp.dot(full_two, up_full, preferred_element_type=jnp.float32) + up_shift.reshape(
        -1
    ).astype(jnp.float32)
    gated = smooth_gate(hidden).astype(jnp.bfloat16)
    piece = gated
    output = (
        middle
        + lax.psum_scatter(
            jnp.dot(piece, down_full, preferred_element_type=jnp.float32).astype(jnp.bfloat16),
            "tensor",
            scatter_dimension=0,
            tiled=True,
        ).astype(jnp.float32)
        + down_shift
    )
    grad_full = lax.all_gather(cotangent, "tensor", axis=0, tiled=True)
    grad_gated = jnp.einsum("rd,fd->rf", grad_full, down_full, preferred_element_type=jnp.float32)
    grad_down = jnp.einsum("rf,rd->fd", gated, grad_full, preferred_element_type=jnp.float32)
    gate_value, gate_pull = jax.vjp(smooth_gate, hidden)
    grad_hidden = gate_pull(grad_gated)[0].astype(jnp.bfloat16)
    grad_up = jnp.einsum("rd,rf->df", full_two, grad_hidden, preferred_element_type=jnp.float32)
    grad_up_shift = jnp.sum(grad_hidden.astype(jnp.float32), axis=0).reshape(up_shift.shape)
    piece = grad_hidden
    grad_two = lax.psum_scatter(
        jnp.einsum("rf,df->rd", piece, up_full, preferred_element_type=jnp.float32).astype(
            jnp.bfloat16
        ),
        "tensor",
        scatter_dimension=0,
        tiled=True,
    ).astype(jnp.float32)
    grad_out_rows = cotangent.astype(jnp.float32)
    grad_down_shift = jnp.sum(grad_out_rows, axis=0)
    grad_gain_b = jnp.sum(grad_two * normed_two, axis=0)
    grad_shift_b = jnp.sum(grad_two, axis=0)
    grad_middle = grad_out_rows + norm_backward(grad_two, normed_two, inverse_two, gain_b)
    grad_out_shift = jnp.sum(grad_middle, axis=0)
    grad_low = grad_middle.astype(jnp.bfloat16)
    grad_gathered = lax.all_gather(grad_low, "tensor", axis=0, tiled=True)
    grad_w_out = jnp.einsum(
        "rc,rd->cd", attended, grad_gathered, preferred_element_type=jnp.float32
    )
    grad_attended = jnp.einsum(
        "rd,cd->rc", grad_gathered, out_full, preferred_element_type=jnp.float32
    ).astype(jnp.bfloat16)
    grad_heads = split_heads(grad_attended)
    grad_keys = jnp.zeros((sequences, length, local_heads, HD), jnp.float32)
    grad_values = jnp.zeros((sequences, length, local_heads, HD), jnp.float32)
    grad_queries = []
    for number, q_start in enumerate(starts):
        q_end = q_start + qblock
        query_block = query[:, q_start:q_end]
        scores = block_scores(query_block, keys[:, :q_end], slopes, q_start, scale)
        probs = jnp.exp(scores - log_sums[number])
        grad_block = grad_heads[:, q_start:q_end]
        grad_values = grad_values.at[:, :q_end].add(
            jnp.einsum(
                "shqk,sqhd->skhd",
                probs.astype(jnp.bfloat16),
                grad_block,
                preferred_element_type=jnp.float32,
            )
        )
        grad_probs = jnp.einsum(
            "sqhd,skhd->shqk", grad_block, values[:, :q_end], preferred_element_type=jnp.float32
        )
        inner = jnp.sum(probs * grad_probs, axis=-1, keepdims=True)
        grad_scores = (probs * (grad_probs - inner)).astype(jnp.bfloat16)
        grad_queries.append(
            scale
            * jnp.einsum(
                "shqk,skhd->sqhd", grad_scores, keys[:, :q_end], preferred_element_type=jnp.float32
            )
        )
        grad_keys = grad_keys.at[:, :q_end].add(
            scale
            * jnp.einsum(
                "shqk,sqhd->skhd", grad_scores, query_block, preferred_element_type=jnp.float32
            )
        )
    grad_query_all = jnp.concatenate(grad_queries, axis=1)
    grad_qkv_rows = (
        jnp.stack([grad_query_all, grad_keys, grad_values])
        .reshape(3, group, width)
        .astype(jnp.bfloat16)
    )
    grad_w_qkv = jnp.einsum(
        "rd,cre->cde", full_one, grad_qkv_rows, preferred_element_type=jnp.float32
    )
    grad_qv_shift = jnp.stack(
        [
            jnp.sum(grad_qkv_rows[0].astype(jnp.float32), axis=0),
            jnp.sum(grad_qkv_rows[2].astype(jnp.float32), axis=0),
        ]
    ).reshape(2, local_heads, HD)
    piece = grad_qkv_rows
    grad_one = lax.psum_scatter(
        jnp.einsum("cre,cde->rd", piece, qkv_full, preferred_element_type=jnp.float32).astype(
            jnp.bfloat16
        ),
        "tensor",
        scatter_dimension=0,
        tiled=True,
    ).astype(jnp.float32)
    grad_gain_a = jnp.sum(grad_one * normed_one, axis=0)
    grad_shift_a = jnp.sum(grad_one, axis=0)
    grad_inputs = grad_middle + norm_backward(grad_one, normed_one, inverse_one, gain_a)
    summed_qkv, summed_qv, summed_out, summed_up, summed_up_shift, summed_down = (
        lax.psum_scatter(
            grad_w_qkv.astype(jnp.bfloat16), "dp", scatter_dimension=1, tiled=True
        ).astype(jnp.float32),
        lax.psum_scatter(
            grad_qv_shift.astype(jnp.bfloat16), "dp", scatter_dimension=2, tiled=True
        ).astype(jnp.float32),
        lax.psum_scatter(
            grad_w_out.astype(jnp.bfloat16), "dp", scatter_dimension=1, tiled=True
        ).astype(jnp.float32),
        lax.psum_scatter(
            grad_up.astype(jnp.bfloat16), "dp", scatter_dimension=0, tiled=True
        ).astype(jnp.float32),
        lax.psum_scatter(
            grad_up_shift.astype(jnp.bfloat16), "dp", scatter_dimension=1, tiled=True
        ).astype(jnp.float32),
        lax.psum_scatter(
            grad_down.astype(jnp.bfloat16), "dp", scatter_dimension=1, tiled=True
        ).astype(jnp.float32),
    )
    sum_gain_a, sum_shift_a, sum_out_shift, sum_gain_b, sum_shift_b, sum_down_shift = (
        lax.psum_scatter(grad_gain_a, ("dp", "tensor"), scatter_dimension=0, tiled=True),
        lax.psum_scatter(grad_shift_a, ("dp", "tensor"), scatter_dimension=0, tiled=True),
        lax.psum_scatter(grad_out_shift, ("dp", "tensor"), scatter_dimension=0, tiled=True),
        lax.psum_scatter(grad_gain_b, ("dp", "tensor"), scatter_dimension=0, tiled=True),
        lax.psum_scatter(grad_shift_b, ("dp", "tensor"), scatter_dimension=0, tiled=True),
        lax.psum_scatter(grad_down_shift, ("dp", "tensor"), scatter_dimension=0, tiled=True),
    )
    return (
        output.astype(jnp.bfloat16),
        grad_inputs.astype(jnp.bfloat16),
        sum_gain_a,
        sum_shift_a,
        summed_qkv,
        summed_qv,
        summed_out,
        sum_out_shift,
        sum_gain_b,
        sum_shift_b,
        summed_up,
        summed_up_shift,
        summed_down,
        sum_down_shift,
    )


def solution(mesh):
    return jax.shard_map(
        local,
        mesh=mesh,
        in_specs=(
            P(("dp", "tensor"), None),
            P(("dp", "tensor")),
            P(("dp", "tensor")),
            P(None, "dp", "tensor"),
            P(None, "tensor", "dp"),
            P("tensor", "dp"),
            P(("dp", "tensor")),
            P(("dp", "tensor")),
            P(("dp", "tensor")),
            P("dp", "tensor"),
            P("tensor", "dp"),
            P("tensor", "dp"),
            P(("dp", "tensor")),
            P(("dp", "tensor"), None),
        ),
        out_specs=(
            P(("dp", "tensor"), None),
            P(("dp", "tensor"), None),
            P(("dp", "tensor")),
            P(("dp", "tensor")),
            P(None, "dp", "tensor"),
            P(None, "tensor", "dp"),
            P("tensor", "dp"),
            P(("dp", "tensor")),
            P(("dp", "tensor")),
            P(("dp", "tensor")),
            P("dp", "tensor"),
            P("tensor", "dp"),
            P("tensor", "dp"),
            P(("dp", "tensor")),
        ),
        check_vma=False,
    )
```

profile of v0, /device:TPU:0, one launch (start us, length us, event | category | flops | bytes accessed | tf_op | source)
XLA Modules:
  0.0 897.3 jit_solution(4286123311036064950)
XLA Ops:
  14.6 42.3 %all-reduce.18 = (f32[1024]{0:T(1024)S(1)}, f32[1024]{0:T(1024)S(1)}, f32[1024]{0:T(1024)S(1)}, f32[1024]{0:T(1024)S(1)}, f32[1024]{0:T(1024)S(1)}) all-reduce(f32[1024]{0:T(1024)S(1)} %dynamic-update-slice.14, f32[1024]{0:T(1024)S(1)} %dynamic-update-slice.13, ...), channel_id=1, replica_groups=mesh['dp'=16,'tensor'=2] {'dp','tensor'}, use_global_device_ids=true, to_apply=%add.6 | all-reduce | flops 5120 | bytes 40960
  64.0 21.3 %all_gather.52 = bf16[2,8,64]{1,0,2:T(2,128)(2,1)S(1)} all-gather(bf16[2,8,4]{1,0,2:T(2,128)(2,1)S(1)} %copy.50), channel_id=1, replica_groups=mesh['dp'=16,'tensor'=2] {'dp'}, dimensions={2}, use_global_device_ids=true | all-gather | bytes 2176 | tf_op jit(solution)/shard_map/all_gather | solution.py:71
  85.8 6.9 all-gather.9.cloned.1.call-done
  92.7 47.4 %all-gather.11.cloned.1.call-done = bf16[3,1024,512]{2,1,0:T(8,128)(2,1)} async-done(((bf16[3,64,512]{2,1,0:T(8,128)(2,1)}), bf16[3,1024,512]{2,1,0:T(8,128)(2,1)}) %all-gather.11.cloned.1.call-update) | async-done | bytes 3145744 | tf_op jit(solution)/shard_map/all_gather | solution.py:70
  140.1 6.0 fusion.19
  169.1 10.0 %all-gather.13.cloned.1.call-done = bf16[512,1024]{0,1:T(8,128)(2,1)} async-done(((bf16[512,64]{0,1:T(8,128)(2,1)}), bf16[512,1024]{0,1:T(8,128)(2,1)}) %all-gather.13.cloned.1.call-update) | async-done | bytes 1048592 | tf_op jit(solution)/shard_map/all_gather | solution.py:72
  183.7 30.2 %reduce-scatter.10.cloned.1.call-done = bf16[512,1024]{1,0:T(8,128)(2,1)} async-done(((bf16[1024,1024]{1,0:T(8,128)(2,1)}), bf16[512,1024]{1,0:T(8,128)(2,1)}) %reduce-scatter.10.cloned.1.call-update) | async-done | bytes 1048592 | tf_op jit(solution)/shard_map/reduce_scatter | solution.py:124
  220.7 22.0 %all_gather.59 = bf16[16,128]{0,1:T(8,128)(2,1)S(1)} all-gather(bf16[16,8]{0,1:T(8,128)(2,1)S(1)} %copy-done.24), channel_id=1, replica_groups=mesh['dp'=16,'tensor'=2] {'dp'}, dimensions={1}, use_global_device_ids=true | all-gather | bytes 4352 | tf_op jit(solution)/shard_map/all_gather | solution.py:74
  242.7 24.2 %all-gather.17.cloned.1.call-done = bf16[1024,2048]{1,0:T(8,128)(2,1)} async-done(((bf16[64,2048]{1,0:T(8,128)(2,1)}), bf16[1024,2048]{1,0:T(8,128)(2,1)}) %all-gather.17.cloned.1.call-update) | async-done | bytes 4194320 | tf_op jit(solution)/shard_map/all_gather | solution.py:73
  266.9 33.7 %all-gather.15.cloned.1.call-done = bf16[1024,1024]{1,0:T(8,128)(2,1)} async-done(((bf16[512,1024]{1,0:T(8,128)(2,1)}), bf16[1024,1024]{1,0:T(8,128)(2,1)}) %all-gather.15.cloned.1.call-update) | async-done | bytes 2097168 | tf_op jit(solution)/shard_map/all_gather | solution.py:134
  300.6 10.9 %fusion.77 = f32[1024,2048]{1,0:T(8,128)} fusion(bf16[1024,1024]{1,0:T(8,128)(2,1)} %all-gather.15.cloned.1.call-done, bf16[1024,2048]{1,0:T(8,128)(2,1)} %all-gather.17.cloned.1.call-done), kind=kOutput, calls=%fused_computation.147 | convolution fusion | flops 4294967296 | bytes 14680064 | tf_op jit(solution)/shard_map/dot_general | solution.py:135
  311.5 23.9 %all-gather.21.cloned.1.call-done = bf16[1024,1024]{1,0:T(8,128)(2,1)} async-done(((bf16[512,1024]{1,0:T(8,128)(2,1)}), bf16[1024,1024]{1,0:T(8,128)(2,1)}) %all-gather.21.cloned.1.call-update) | async-done | bytes 2097168 | tf_op jit(solution)/shard_map/all_gather | solution.py:150
  335.3 53.0 %all-gather.19.cloned.1.call-done = bf16[2048,1024]{0,1:T(8,128)(2,1)} async-done(((bf16[2048,64]{0,1:T(8,128)(2,1)}), bf16[2048,1024]{0,1:T(8,128)(2,1)}) %all-gather.19.cloned.1.call-update) | async-done | bytes 4194320 | tf_op jit(solution)/shard_map/all_gather | solution.py:75
  388.3 13.1 %fusion.67 = (bf16[2048]{0:T(1024)(128)(2,1)S(1)}, bf16[1024,2048]{1,0:T(8,128)(2,1)S(1)}) fusion(f32[1024,2048]{1,0:T(8,128)} %fusion.77, f32[2048]{0:T(1024)S(1)} %bitcast_convert_fusion.1, bf16[1024,1024]{1,0:T(8,128)(2,1)} %all-gather.21.cloned.1.call-done, bf16[2048,1024]{0,1:T(8,128)(2,1)} %all-gather.19.cloned.1.call-done), kind=kOutput, calls=%fused_computation.138 | convolution fusion | flops 4341102592 | bytes 18886656 | tf_op jit(solution)/shard_map/rd,fd->rf/dot_general | solution.py:151
  409.4 30.3 %reduce-scatter.14.cloned.1.call-done = bf16[512,1024]{1,0:T(8,128)(2,1)} async-done(((bf16[1024,1024]{1,0:T(8,128)(2,1)}), bf16[512,1024]{1,0:T(8,128)(2,1)}) %reduce-scatter.14.cloned.1.call-update) | async-done | bytes 1048592 | tf_op jit(solution)/shard_map/reduce_scatter | solution.py:158
  447.5 10.8 %convolution_convert_fusion = bf16[2048,1024]{0,1:T(8,128)(2,1)} fusion(bf16[1024,1024]{1,0:T(8,128)(2,1)} %all-gather.21.cloned.1.call-done, f32[1024,2048]{1,0:T(8,128)} %fusion.77, f32[2048]{0:T(1024)S(1)} %bitcast_convert_fusion.1), kind=kOutput, calls=%fused_computation.34 | convolution fusion | flops 4318035968 | bytes 14688256 | tf_op jit(solution)/shard_map/rf,rd->fd/dot_general | solution.py:152
  458.6 9.5 %convolution_convert_fusion.1 = bf16[1024,2048]{1,0:T(8,128)(2,1)} fusion(bf16[1024,1024]{1,0:T(8,128)(2,1)} %all-gather.15.cloned.1.call-done, bf16[1024,2048]{1,0:T(8,128)(2,1)} %copy-done.29), kind=kOutput, calls=%fused_computation.35 | convolution fusion | flops 4297064448 | bytes 10485760 | tf_op jit(solution)/shard_map/rd,rf->df/dot_general | solution.py:155
  468.1 12.6 %all-gather.23.cloned.1.call-done = bf16[1024,1024]{1,0:T(8,128)(2,1)} async-done(((bf16[512,1024]{1,0:T(8,128)(2,1)}), bf16[1024,1024]{1,0:T(8,128)(2,1)}) %all-gather.23.cloned.1.call-update) | async-done | bytes 2097168 | tf_op jit(solution)/shard_map/all_gather | solution.py:173
  489.3 8.2 multiply_reduce_fusion.1
  505.0 6.8 multiply_convert_fusion.1
  516.1 14.2 %multiply_reduce_fusion = (f32[8,512]{1,0:T(8,128)S(1)}, f32[8,512,1024]{2,1,0:T(8,128)}) fusion(f32[8,512,1024]{2,1,0:T(8,128)} %copy-done, f32[8,512]{1,0:T(8,128)S(1)} %log_add_fusion, bf16[1024,8,64]{0,2,1:T(8,128)(2,1)} %bitcast.142, bf16[1,1024,8,64]{1,3,2,0:T(8,128)(2,1)} %bitcast.156), kind=kOutput, calls=%fused_computation.1 | convolution fusion | flops 549449728 | bytes 35160064 | tf_op jit(solution)/shard_map/sqhd,skhd->shqk/dot_general | solution.py:198
  531.9 7.9 multiply_convert_fusion
  549.0 6.5 fusion.76
  559.1 7.7 convert_bitcast_fusion
  566.7 7.7 copy.62
  578.9 7.8 bitcast_convert_fusion
  586.8 11.8 %convolution_convert_fusion.3 = bf16[1024,1024]{1,0:T(8,128)(2,1)} fusion(bf16[2048,1024]{0,1:T(8,128)(2,1)} %all-gather.19.cloned.1.call-done, f32[1024,2048]{1,0:T(8,128)} %fusion.77, f32[2048]{0:T(1024)S(1)} %bitcast_convert_fusion.1), kind=kOutput, calls=%fused_computation.86 | convolution fusion | flops 4316987392 | bytes 14688256 | tf_op jit(solution)/shard_map/dot_general | solution.py:143
  601.8 62.9 %all-reduce.19 = (bf16[2,8,64]{1,2,0:T(8,128)(2,1)S(1)}, bf16[16,128]{1,0:T(8,128)(2,1)S(1)}) all-reduce(bf16[2,8,64]{1,2,0:T(8,128)(2,1)S(1)} %copy.63, bf16[16,128]{1,0:T(8,128)(2,1)S(1)} %bitcast.162), channel_id=9, replica_groups=mesh['dp'=16,'tensor'=2] {'dp'}, use_global_device_ids=true, to_apply=%region_25.26.clone | all-reduce | flops 3072 | bytes 12288
  669.6 77.4 %all-reduce.22.cloned.1.call-done = bf16[3,1024,512]{2,0,1:T(4,128)(2,1)} async-done(((bf16[3,1024,512]{2,0,1:T(4,128)(2,1)}), bf16[3,1024,512]{2,0,1:T(4,128)(2,1)}) %all-reduce.22.cloned.1.call-update) | async-done | bytes 3145744
  748.9 59.0 %reduce-scatter.18.cloned.1.call-done = bf16[512,64]{0,1:T(8,128)(2,1)} async-done(((bf16[512,1024]{0,1:T(8,128)(2,1)}), bf16[512,64]{0,1:T(8,128)(2,1)}) %reduce-scatter.18.cloned.1.call-update) | async-done | bytes 65552 | tf_op jit(solution)/shard_map/reduce_scatter | solution.py:249
  809.4 31.5 %reduce-scatter.16.cloned.1.call-done = bf16[512,1024]{1,0:T(8,128)(2,1)} async-done(((bf16[1024,1024]{1,0:T(8,128)(2,1)}), bf16[512,1024]{1,0:T(8,128)(2,1)}) %reduce-scatter.16.cloned.1.call-update) | async-done | bytes 1048592 | tf_op jit(solution)/shard_map/reduce_scatter | solution.py:231
  843.1 40.1 %all-reduce.17 = (f32[1024]{0:T(1024)S(1)}, f32[1024]{0:T(1024)S(1)}, f32[1024]{0:T(1024)S(1)}, f32[1024]{0:T(1024)S(1)}, f32[1024]{0:T(1024)S(1)}, /*index=5*/f32[1024]{0:T(1024)S(1)}, f32[1024]{0:T(1024)S(1)}) all-reduce(f32[1024]{0:T(1024)S(1)} %dynamic-update-slice.15, ...), channel_id=1, replica_groups=mesh['dp'=16,'tensor'=2] {'dp','tensor'}, use_global_device_ids=true, to_apply=%add.7 | all-reduce | flops 7168 | bytes 57344
  (200 shorter events, 123.1 us)
Async XLA Ops:
  7.2 85.5 %all-gather.9.cloned.1.call-start = ((), (), s32[]{:S(2)}) async-start(), calls=%async_computation.7 | async-start | bytes 3145728 | tf_op jit(solution)/shard_map/all_gather | solution.py:92
  8.7 55.2 %copy-start.18 = (f32[512]{0:T(512)}, f32[512]{0:T(512)S(1)}, u32[]{:S(2)}) copy-start(f32[512]{0:T(512)S(1)} %broadcast_multiply_fusion.5) | copy-start | bytes 6148
  8.7 55.3 %copy-start.25 = (bf16[2,8,4]{1,2,0:T(4,128)(2,1)S(1)}, bf16[2,8,4]{1,2,0:T(4,128)(2,1)}, u32[]{:S(2)}) copy-start(bf16[2,8,4]{1,2,0:T(4,128)(2,1)} %param.30) | copy-start | bytes 388
  10.3 135.7 %copy-start.22 = (f32[512]{0:T(512)}, f32[512]{0:T(512)S(1)}, u32[]{:S(2)}) copy-start(f32[512]{0:T(512)S(1)} %add_rsqrt_fusion.1) | copy-start | bytes 6148
  59.5 80.6 %all-gather.11.cloned.1.call-start = ((), (), s32[]{:S(2)}) async-start(), calls=%async_computation.8 | async-start | bytes 3342336 | tf_op jit(solution)/shard_map/all_gather | solution.py:70
  60.3 118.8 %all-gather.13.cloned.1.call-start = ((), (), s32[]{:S(2)}) async-start(), calls=%async_computation.9 | async-start | bytes 1114112 | tf_op jit(solution)/shard_map/all_gather | solution.py:72
  61.0 152.9 %reduce-scatter.10.cloned.1.call-start = ((), (), s32[]{:S(2)}) async-start(), calls=%async_computation.10 | async-start | bytes 3145728 | tf_op jit(solution)/shard_map/reduce_scatter | solution.py:124
  146.4 16.5 %copy-start.7 = (bf16[1,1024,512]{1,2,0:T(8,128)(2,1)}, bf16[1,1024,512]{1,2,0:T(8,128)(2,1)S(1)}, u32[]{:S(2)}) copy-start(bf16[1,1024,512]{1,2,0:T(8,128)(2,1)S(1)} %get-tuple-element.148) | copy-start | bytes 3145732
  169.0 14.0 %copy-start.15 = (bf16[1,1024,8,64]{1,3,2,0:T(8,128)(2,1)}, bf16[1,1024,8,64]{1,3,2,0:T(8,128)(2,1)S(1)}, u32[]{:S(2)}) copy-start(bf16[1,1024,8,64]{1,3,2,0:T(8,128)(2,1)S(1)} %pad_maximum_fusion.3) | copy-start | bytes 3145732
  179.1 34.9 %copy-start.2 = (bf16[512,1024]{1,0:T(8,128)(2,1)S(1)}, bf16[512,1024]{1,0:T(8,128)(2,1)}, u32[]{:S(2)}) copy-start(bf16[512,1024]{1,0:T(8,128)(2,1)} %param.26) | copy-start | bytes 3145732
  183.1 83.8 %all-gather.17.cloned.1.call-start = ((), (), s32[]{:S(2)}) async-start(), calls=%async_computation.12 | async-start | bytes 4456448 | tf_op jit(solution)/shard_map/all_gather | solution.py:73
  183.7 116.9 %all-gather.15.cloned.1.call-start = ((), (), s32[]{:S(2)}) async-start(), calls=%async_computation.11 | async-start | bytes 3145728 | tf_op jit(solution)/shard_map/all_gather | solution.py:134
  219.1 116.2 %all-gather.21.cloned.1.call-start = ((), (), s32[]{:S(2)}) async-start(), calls=%async_computation.15 | async-start | bytes 3145728 | tf_op jit(solution)/shard_map/all_gather | solution.py:150
  219.9 168.5 %all-gather.19.cloned.1.call-start = ((), (), s32[]{:S(2)}) async-start(), calls=%async_computation.13 | async-start | bytes 4456448 | tf_op jit(solution)/shard_map/all_gather | solution.py:75
  220.6 219.1 %reduce-scatter.14.cloned.1.call-start = ((), (), s32[]{:S(2)}) async-start(), calls=%async_computation.16 | async-start | bytes 3145728 | tf_op jit(solution)/shard_map/reduce_scatter | solution.py:158
  388.3 15.1 %copy-start.26 = (bf16[1024,2048]{1,0:T(8,128)(2,1)S(1)}, bf16[1024,2048]{1,0:T(8,128)(2,1)}, u32[]{:S(2)}) copy-start(bf16[1024,2048]{1,0:T(8,128)(2,1)} %all-gather.17.cloned.1.call-done) | copy-start | bytes 12582916
  409.2 71.5 %all-gather.23.cloned.1.call-start = ((), (), s32[]{:S(2)}) async-start(), calls=%async_computation.17 | async-start | bytes 3145728 | tf_op jit(solution)/shard_map/all_gather | solution.py:173
  447.5 218.6 %reduce-scatter.22.cloned.1.call-start = ((), (), s32[]{:S(2)}) async-start(), calls=%async_computation.21 | async-start | bytes 4456448 | tf_op jit(solution)/shard_map/reduce_scatter | solution.py:258
  458.3 209.5 %reduce-scatter.20.cloned.1.call-start = ((), (), s32[]{:S(2)}) async-start(), calls=%async_computation.20 | async-start | bytes 4456448 | tf_op jit(solution)/shard_map/reduce_scatter | solution.py:252
  468.1 279.0 %all-reduce.22.cloned.1.call-start = ((), (), s32[]{:S(2)}) async-start(), calls=%async_computation.22 | async-start | bytes 8388608
  480.7 16.8 %slice-start = ((s8[16777216]{0:T(1024)(128)(4,1)}), s8[4194304]{0:T(1024)(128)(4,1)S(1)}, s32[]{:S(2)}) async-start(s8[16777216]{0:T(1024)(128)(4,1)} %bitcast.136), calls=%async_computation.23 | async-start | bytes 8388608
  513.8 16.6 %slice-start.4 = ((s8[16777216]{0:T(1024)(128)(4,1)}), s8[4194304]{0:T(1024)(128)(4,1)S(1)}, s32[]{:S(2)}) async-start(s8[16777216]{0:T(1024)(128)(4,1)} %bitcast.138), calls=%async_computation.27 | async-start | bytes 8388608
  516.1 14.2 %slice-start.5 = ((s8[16777216]{0:T(1024)(128)(4,1)}), s8[4194304]{0:T(1024)(128)(4,1)S(1)}, s32[]{:S(2)}) async-start(s8[16777216]{0:T(1024)(128)(4,1)} %bitcast.138), calls=%async_computation.28 | async-start | bytes 8388608
  516.1 14.3 %slice-start.6 = ((s8[16777216]{0:T(1024)(128)(4,1)}), s8[4194304]{0:T(1024)(128)(4,1)S(1)}, s32[]{:S(2)}) async-start(s8[16777216]{0:T(1024)(128)(4,1)} %bitcast.138), calls=%async_computation.29 | async-start | bytes 8388608
  516.1 15.8 %slice-start.7 = ((s8[16777216]{0:T(1024)(128)(4,1)}), s8[4194304]{0:T(1024)(128)(4,1)S(1)}, s32[]{:S(2)}) async-start(s8[16777216]{0:T(1024)(128)(4,1)} %bitcast.138), calls=%async_computation.30 | async-start | bytes 8388608
  574.5 233.4 %reduce-scatter.18.cloned.1.call-start = ((), (), s32[]{:S(2)}) async-start(), calls=%async_computation.19 | async-start | bytes 1114112 | tf_op jit(solution)/shard_map/reduce_scatter | solution.py:249
  578.9 262.0 %reduce-scatter.16.cloned.1.call-start = ((), (), s32[]{:S(2)}) async-start(), calls=%async_computation.18 | async-start | bytes 3145728 | tf_op jit(solution)/shard_map/reduce_scatter | solution.py:231
  586.8 14.5 %copy-start.27 = (f32[32]{0:T(128)S(1)}, f32[32]{0:T(128)}, u32[]{:S(2)}) copy-start(f32[32]{0:T(128)} %param.38) | copy-start | bytes 388
  586.8 299.9 %reduce-scatter.12.cloned.1.call-start = ((), (), s32[]{:S(2)}) async-start(), calls=%async_computation.14 | async-start | bytes 3145728 | tf_op jit(solution)/shard_map/reduce_scatter | solution.py:142
  598.7 242.2 %copy-start.19 = (f32[512]{0:T(512)S(1)}, f32[512]{0:T(512)}, u32[]{:S(2)}) copy-start(f32[512]{0:T(512)} %copy-done.18) | copy-start | bytes 6148
  598.7 242.2 %copy-start.21 = (f32[1024]{0:T(1024)S(1)}, f32[1024]{0:T(1024)}, u32[]{:S(2)}) copy-start(f32[1024]{0:T(1024)} %copy-done.20) | copy-start | bytes 12292
  598.7 242.2 %copy-start.23 = (f32[512]{0:T(512)S(1)}, f32[512]{0:T(512)}, u32[]{:S(2)}) copy-start(f32[512]{0:T(512)} %copy-done.22) | copy-start | bytes 6148
  (22 other events, 138.8 us)
Sparse Core Ops, SparseCore 0:
  59.7 32.9 all-gather.8
  94.8 45.2 all-gather.10
  142.3 36.7 all-gather.12
  183.2 30.7 reduce-scatter.9
  216.2 50.6 all-gather.16
  268.9 31.5 all-gather.14
  302.2 33.1 all-gather.20
  337.7 50.5 all-gather.18
  409.3 30.3 reduce-scatter.13
  447.6 33.0 all-gather.22
  484.6 72.4 reduce-scatter.21
  561.3 71.7 reduce-scatter.19
  636.7 110.2 all-reduce.21
  751.6 56.2 reduce-scatter.17
  810.0 30.8 reduce-scatter.15
  843.0 32.4 reduce-scatter.11
where the time goes:
time: 902 us; the launch traced here: 897 us
  waiting for transfers between devices  444 us (49%)
  blocking collectives  189 us (21%)
  matrix products  154 us (17%)
  other arithmetic  53.6 us (6%)
  local copies, waits for them, and re-layouts  39.6 us (4%)
  between operations  16.7 us (2%)
    unnamed x3, blocking collectives  145 us
    unnamed x17, waiting for transfers between devices  80.9 us
    reduce_scatter x1, waiting for transfers between devices, local(): lax.psum_scatter(grad_w_out.astype(jnp.bfloat16), 'dp', scatter_dimension...  59 us
    all_gather x1, waiting for transfers between devices, local(): lax.all_gather(w_down, 'dp', axis=1, tiled=True)  53 us
    all_gather x1, waiting for transfers between devices, local(): lax.all_gather(w_qkv, 'dp', axis=1, tiled=True)  47.4 us
    all_gather x1, waiting for transfers between devices, local(): full_two = lax.all_gather(low_two, 'tensor', axis=0, tiled=True)  33.7 us
    reduce_scatter x1, waiting for transfers between devices, local(): lax.psum_scatter(jnp.einsum('cre,cde->rd', piece, qkv_full, preferred_ele...  31.5 us
    reduce_scatter x1, waiting for transfers between devices, local(): lax.psum_scatter(jnp.einsum('rf,df->rd', piece, up_full, preferred_elemen...  30.3 us
  transfers between devices with their start and end apart: 16, of which 13 were waited for; matrix products, arithmetic and copies ran while one was open for 21% of the time, Pallas kernels for 0%

commit v1 on v0

v1 whole, which is shorter than its diff:
```python
import functools
import math

import jax
import jax.numpy as jnp
from jax import lax
from jax.experimental import pallas as pl
from jax.experimental.pallas import tpu as pltpu
from jax.sharding import PartitionSpec as P

H = 16
HD = 64
SEQ_LEN = 1024
PAIR = 2 * HD
QB = 256

EPSILON = 1e-05
MASKED = -1e30
F32 = jnp.float32
BF16 = jnp.bfloat16


def normalize(values):
    centred = values - jnp.mean(values, axis=-1, keepdims=True)
    inverse = lax.rsqrt(jnp.mean(centred * centred, axis=-1, keepdims=True) + EPSILON)
    return (centred * inverse, inverse)


def norm_backward(grad, normed, inverse, gain):
    scaled = grad * gain
    return inverse * (
        scaled
        - jnp.mean(scaled, axis=-1, keepdims=True)
        - normed * jnp.mean(scaled * normed, axis=-1, keepdims=True)
    )


def smooth_gate(values):
    return jax.nn.gelu(values, approximate=True)


def mm(a, b):
    return lax.dot_general(a, b, (((1,), (0,)), ((), ())), preferred_element_type=F32)


def mm_t(a, b):
    return lax.dot_general(a, b, (((1,), (1,)), ((), ())), preferred_element_type=F32)


def t_mm(a, b):
    return lax.dot_general(a, b, (((0,), (0,)), ((), ())), preferred_element_type=F32)


def head_masked(values, head):
    lane = lax.broadcasted_iota(jnp.int32, values.shape, 1)
    return jnp.where(lane // HD == head, values, jnp.zeros_like(values))


def stored_row(flip, position, length):
    half = length // 2
    return pl.multiple_of(((position // half + flip) % 2) * half + position % half, QB)


def attend_kernel(flip_ref, slope_ref, q_ref, k_ref, v_ref, o_ref, k_all, v_all):
    length = q_ref.shape[0]
    half = length // 2
    flip = flip_ref[0]
    first = pl.program_id(1) * 2
    for number in range(2):
        rows = pl.ds(stored_row(flip, number * half, length), half)
        k_all[number * half : (number + 1) * half] = k_ref[rows, :]
        v_all[number * half : (number + 1) * half] = v_ref[rows, :]
    for start in range(0, length, QB):
        end = start + QB
        q = q_ref[pl.ds(stored_row(flip, start, length), QB), :]
        q = (q.astype(F32) * (1.0 / math.sqrt(HD))).astype(BF16)
        offset = (
            lax.broadcasted_iota(jnp.int32, (1, end), 1) - start
        ).astype(F32)
        row = lax.broadcasted_iota(jnp.int32, (QB, QB), 0)
        col = lax.broadcasted_iota(jnp.int32, (QB, QB), 1)
        outs = []
        for head in range(2):
            scores = mm_t(head_masked(q, head), k_all[:end]) + slope_ref[first + head] * offset
            diagonal = jnp.where(col <= row, scores[:, start:], MASKED)
            scores = (
                jnp.concatenate([scores[:, :start], diagonal], axis=1) if start else diagonal
            )
            top = jnp.max(scores, axis=-1, keepdims=True)
            exponent = jnp.exp(scores - top)
            total = jnp.sum(exponent, axis=-1, keepdims=True)
            outs.append(mm(exponent.astype(BF16), v_all[:end]) / total)
        lane = lax.broadcasted_iota(jnp.int32, (QB, PAIR), 1)
        o_ref[pl.ds(stored_row(flip, start, length), QB), :] = jnp.where(
            lane < HD, outs[0], outs[1]
        ).astype(BF16)


def attend_back_kernel(
    flip_ref, slope_ref, q_ref, k_ref, v_ref, g_ref, dq_ref, dk_ref, dv_ref, k_all, v_all, dk, dv
):
    length = q_ref.shape[0]
    half = length // 2
    flip = flip_ref[0]
    first = pl.program_id(1) * 2
    for number in range(2):
        rows = pl.ds(stored_row(flip, number * half, length), half)
        k_all[number * half : (number + 1) * half] = k_ref[rows, :]
        v_all[number * half : (number + 1) * half] = v_ref[rows, :]
    for start in reversed(range(0, length, QB)):
        end = start + QB
        here = pl.ds(stored_row(flip, start, length), QB)
        q = (q_ref[here, :].astype(F32) * (1.0 / math.sqrt(HD))).astype(BF16)
        g = g_ref[here, :]
        offset = (lax.broadcasted_iota(jnp.int32, (end, 1), 0) - start).astype(F32)
        key = lax.broadcasted_iota(jnp.int32, (QB, QB), 0)
        query = lax.broadcasted_iota(jnp.int32, (QB, QB), 1)
        dq_sum = None
        dk_sum = None
        dv_sum = None
        for head in range(2):
            q_head = head_masked(q, head)
            g_head = head_masked(g, head)
            scores = mm_t(k_all[:end], q_head) + slope_ref[first + head] * offset
            diagonal = jnp.where(key <= query, scores[start:], MASKED)
            scores = (
                jnp.concatenate([scores[:start], diagonal], axis=0) if start else diagonal
            )
            top = jnp.max(scores, axis=0, keepdims=True)
            exponent = jnp.exp(scores - top)
            probs = exponent * (1.0 / jnp.sum(exponent, axis=0, keepdims=True))
            grad_probs = mm_t(v_all[:end], g_head)
            inner = jnp.sum(probs * grad_probs, axis=0, keepdims=True)
            grad_scores = (probs * (grad_probs - inner)).astype(BF16)
            dq_part = t_mm(grad_scores, head_masked(k_all[:end], head))
            dk_part = mm(grad_scores, q_head)
            dv_part = mm(probs.astype(BF16), g_head)
            dq_sum = dq_part if dq_sum is None else dq_sum + dq_part
            dk_sum = dk_part if dk_sum is None else dk_sum + dk_part
            dv_sum = dv_part if dv_sum is None else dv_sum + dv_part
        dq_ref[here, :] = (dq_sum * (1.0 / math.sqrt(HD))).astype(BF16)
        if end == length:
            dk[...] = dk_sum
            dv[...] = dv_sum
        else:
            dk[:end] += dk_sum
            dv[:end] += dv_sum
    for number in range(2):
        rows = pl.ds(stored_row(flip, number * half, length), half)
        dk_ref[rows, :] = dk[number * half : (number + 1) * half].astype(BF16)
        dv_ref[rows, :] = dv[number * half : (number + 1) * half].astype(BF16)


def attention_call(kernel, flip, slopes, operands, n_out, scratch, length, costs):
    group, width = operands[0].shape
    block = pl.BlockSpec((length, PAIR), lambda s, h: (s, h))
    scalar = pl.BlockSpec(memory_space=pltpu.SMEM)
    shape = jax.ShapeDtypeStruct((group, width), BF16)
    return pl.pallas_call(
        kernel,
        grid=(group // length, width // PAIR),
        out_shape=[shape] * n_out,
        in_specs=[scalar, scalar] + [block] * len(operands),
        out_specs=[block] * n_out,
        scratch_shapes=scratch,
        compiler_params=pltpu.CompilerParams(vmem_limit_bytes=48 * 1024 * 1024),
        cost_estimate=costs,
    )(flip, slopes, *operands)


def local(
    tokens,
    gain_one,
    shift_one,
    w_qkv,
    bias_qv,
    w_out,
    bias_out,
    gain_two,
    shift_two,
    w_up,
    bias_up,
    w_down,
    bias_down,
    cotangent,
):
    parts = lax.axis_size("tensor")
    n_dp = lax.axis_size("dp")
    everyone = n_dp * parts
    t_index = lax.axis_index("tensor")
    core = lax.axis_index("dp") % 2
    chips = n_dp // 2
    swap_cores = [(i, i ^ 1) for i in range(n_dp)]
    same_core = [list(range(c, n_dp, 2)) for c in range(2)]

    def gather_weight(shard):
        rows, columns = shard.shape
        mine = lax.all_gather(shard, "dp", axis=0, axis_index_groups=same_core, tiled=False)
        theirs = lax.ppermute(mine, "dp", swap_cores)
        first = jnp.where(core == 0, mine, theirs)
        second = jnp.where(core == 0, theirs, mine)
        return jnp.stack([first, second], axis=1).reshape(n_dp * rows, columns)

    def scatter_weight(grad):
        rows, columns = grad.shape
        blocks = grad.reshape(chips, 2, rows // n_dp, columns)
        away = lax.dynamic_index_in_dim(blocks, 1 - core, 1, keepdims=False).astype(BF16)
        keep = lax.dynamic_index_in_dim(blocks, core, 1, keepdims=False).astype(F32)
        both = (keep + lax.ppermute(away, "dp", swap_cores).astype(F32)).astype(BF16)
        both = both.reshape(rows // 2, columns)
        return lax.psum_scatter(
            both, "dp", scatter_dimension=0, axis_index_groups=same_core, tiled=True
        ).astype(F32)

    def gather_rows(mine):
        if parts == 2:
            return [mine, lax.ppermute(mine, "tensor", [(0, 1), (1, 0)])]
        return [lax.all_gather(mine, "tensor", axis=0, tiled=True)]

    def scatter_rows(product, blocks):
        if parts == 2:
            sent = lax.ppermute(product(blocks[1]).astype(BF16), "tensor", [(0, 1), (1, 0)])
            return product(blocks[0]) + sent.astype(F32)
        return lax.psum_scatter(
            product(blocks[0]).astype(BF16), "tensor", scatter_dimension=0, tiled=True
        ).astype(F32)

    def joined(blocks):
        return blocks[0] if len(blocks) == 1 else jnp.concatenate(blocks, axis=0)

    def split(rows):
        if parts == 2:
            return [rows[: rows.shape[0] // 2], rows[rows.shape[0] // 2 :]]
        return [rows]

    vec = gain_one.shape[0]
    n_qv = bias_qv.size
    n_bu = bias_up.size
    packed = jnp.concatenate(
        [gain_one, shift_one, bias_out, gain_two, shift_two, bias_down]
        + [bias_qv.astype(F32).reshape(-1), bias_up.astype(F32).reshape(-1)]
    )
    small = lax.all_gather(packed, ("dp", "tensor"), axis=0, tiled=False)
    gain_a, shift_a, out_shift, gain_b, shift_b, down_shift = (
        small[:, n * vec : (n + 1) * vec].reshape(-1) for n in range(6)
    )
    at = 6 * vec
    local_small = lax.dynamic_index_in_dim(
        small.reshape(n_dp, parts, -1), t_index, 1, keepdims=False
    )
    local_heads = bias_qv.shape[1]
    width = local_heads * HD
    qv_shift = (
        local_small[:, at : at + n_qv]
        .reshape(n_dp, 2, local_heads, -1)
        .transpose(1, 2, 0, 3)
        .reshape(2, width)
    )
    up_shift = (
        local_small[:, at + n_qv :]
        .reshape(n_dp, bias_up.shape[0], -1)
        .transpose(1, 0, 2)
        .reshape(-1)
    )
    hidden_units = up_shift.shape[0]

    first_full = gather_weight(
        jnp.concatenate([w_qkv[0], w_qkv[1], w_qkv[2], w_out.T], axis=1)
    )
    up_full = gather_weight(w_up)
    down_t = gather_weight(w_down.T)
    qkv_full = first_full[:, : 3 * width]
    out_t = first_full[:, 3 * width :]

    rows = tokens.shape[0]
    group = rows * parts
    length = min(SEQ_LEN, group)
    sequences = group // length
    head_ids = t_index * local_heads + lax.iota(jnp.int32, local_heads)
    slopes = jnp.exp2(-8.0 * (head_ids + 1).astype(F32) / H)
    flip = (t_index if parts == 2 else 0 * t_index).astype(jnp.int32).reshape(1)

    cot_blocks = gather_rows(cotangent)
    inputs = tokens.astype(F32)
    normed_one, inverse_one = normalize(inputs)
    one_blocks = gather_rows((normed_one * gain_a + shift_a).astype(BF16))
    qkv_shift = jnp.concatenate([qv_shift[0], jnp.zeros((width,), F32), qv_shift[1]])
    qkv_low = joined([(mm(b, qkv_full) + qkv_shift).astype(BF16) for b in one_blocks])
    query, keys, values = (qkv_low[:, n * width : (n + 1) * width] for n in range(3))
    pair_area = sequences * local_heads * length * length
    vmem = pltpu.VMEM((length, PAIR), BF16)
    (attended,) = attention_call(
        attend_kernel,
        flip,
        slopes,
        (query, keys, values),
        1,
        [vmem, vmem],
        length,
        pl.CostEstimate(
            flops=4 * PAIR * pair_area, bytes_accessed=8 * group * width, transcendentals=pair_area
        ),
    )
    middle = (
        inputs + scatter_rows(lambda b: mm_t(b, out_t), split(attended)) + out_shift
    )
    normed_two, inverse_two = normalize(middle)
    two_blocks = gather_rows((normed_two * gain_b + shift_b).astype(BF16))
    hidden = [mm(b, up_full) + up_shift for b in two_blocks]
    gated = [smooth_gate(h).astype(BF16) for h in hidden]
    grad_gated = [mm(c, down_t) for c in cot_blocks]
    grad_hidden = [
        jax.vjp(smooth_gate, h)[1](g)[0].astype(BF16) for h, g in zip(hidden, grad_gated)
    ]
    grad_two = scatter_rows(lambda b: mm_t(b, up_full), grad_hidden)
    output = middle + scatter_rows(lambda b: mm_t(b, down_t), gated) + down_shift

    cot_all = joined(cot_blocks)
    grad_hidden_all = joined(grad_hidden)
    summed_down = scatter_weight(t_mm(cot_all, joined(gated)).astype(BF16))
    summed_up = scatter_weight(t_mm(joined(two_blocks), grad_hidden_all).astype(BF16))
    grad_up_shift = jnp.sum(grad_hidden_all.astype(F32), axis=0)

    grad_out_rows = cotangent.astype(F32)
    grad_down_shift = jnp.sum(grad_out_rows, axis=0)
    grad_gain_b = jnp.sum(grad_two * normed_two, axis=0)
    grad_shift_b = jnp.sum(grad_two, axis=0)
    grad_middle = grad_out_rows + norm_backward(grad_two, normed_two, inverse_two, gain_b)
    grad_out_shift = jnp.sum(grad_middle, axis=0)
    low_blocks = gather_rows(grad_middle.astype(BF16))
    grad_attended = joined([mm(b, out_t).astype(BF16) for b in low_blocks])
    scratch = [vmem, vmem] + [pltpu.VMEM((length, PAIR), F32)] * 2
    grad_qkv_parts = attention_call(
        attend_back_kernel,
        flip,
        slopes,
        (query, keys, values, grad_attended),
        3,
        scratch,
        length,
        pl.CostEstimate(
            flops=10 * PAIR * pair_area,
            bytes_accessed=14 * group * width,
            transcendentals=pair_area,
        ),
    )
    grad_qkv_rows = jnp.concatenate(grad_qkv_parts, axis=1)
    grad_one = scatter_rows(lambda b: mm_t(b, qkv_full), split(grad_qkv_rows))
    grad_first = jnp.concatenate(
        [
            t_mm(joined(one_blocks), grad_qkv_rows).astype(BF16),
            t_mm(joined(low_blocks), attended).astype(BF16),
        ],
        axis=1,
    )
    summed_first = scatter_weight(grad_first)
    grad_qv_shift = jnp.stack(
        [
            jnp.sum(grad_qkv_parts[0].astype(F32), axis=0),
            jnp.sum(grad_qkv_parts[2].astype(F32), axis=0),
        ]
    )
    grad_gain_a = jnp.sum(grad_one * normed_one, axis=0)
    grad_shift_a = jnp.sum(grad_one, axis=0)
    grad_inputs = grad_middle + norm_backward(grad_one, normed_one, inverse_one, gain_a)

    mine = (lax.iota(jnp.int32, parts) == t_index)[None, :, None]

    def placed(values):
        return jnp.where(mine, values.reshape(n_dp, 1, -1), 0.0).reshape(everyone, -1)

    packed_grads = jnp.concatenate(
        [
            v.reshape(everyone, vec)
            for v in (
                grad_gain_a,
                grad_shift_a,
                grad_out_shift,
                grad_gain_b,
                grad_shift_b,
                grad_down_shift,
            )
        ]
        + [
            placed(grad_qv_shift.reshape(2, local_heads, n_dp, -1).transpose(2, 0, 1, 3)),
            placed(grad_up_shift.reshape(bias_up.shape[0], n_dp, -1).transpose(1, 0, 2)),
        ],
        axis=1,
    )
    sums = lax.psum_scatter(
        packed_grads, ("dp", "tensor"), scatter_dimension=0, tiled=True
    ).reshape(-1)
    sum_gain_a, sum_shift_a, sum_out_shift, sum_gain_b, sum_shift_b, sum_down_shift = (
        sums[n * vec : (n + 1) * vec] for n in range(6)
    )
    summed_qkv = jnp.stack([summed_first[:, n * width : (n + 1) * width] for n in range(3)])
    return (
        output.astype(BF16),
        grad_inputs.astype(BF16),
        sum_gain_a,
        sum_shift_a,
        summed_qkv,
        sums[at : at + n_qv].reshape(bias_qv.shape),
        summed_first[:, 3 * width :].T,
        sum_out_shift,
        sum_gain_b,
        sum_shift_b,
        summed_up,
        sums[at + n_qv :].reshape(bias_up.shape),
        summed_down.T,
        sum_down_shift,
    )


def solution(mesh):
    return jax.shard_map(
        local,
        mesh=mesh,
        in_specs=(
            P(("dp", "tensor"), None),
            P(("dp", "tensor")),
            P(("dp", "tensor")),
            P(None, "dp", "tensor"),
            P(None, "tensor", "dp"),
            P("tensor", "dp"),
            P(("dp", "tensor")),
            P(("dp", "tensor")),
            P(("dp", "tensor")),
            P("dp", "tensor"),
            P("tensor", "dp"),
            P("tensor", "dp"),
            P(("dp", "tensor")),
            P(("dp", "tensor"), None),
        ),
        out_specs=(
            P(("dp", "tensor"), None),
            P(("dp", "tensor"), None),
            P(("dp", "tensor")),
            P(("dp", "tensor")),
            P(None, "dp", "tensor"),
            P(None, "tensor", "dp"),
            P("tensor", "dp"),
            P(("dp", "tensor")),
            P(("dp", "tensor")),
            P(("dp", "tensor")),
            P("dp", "tensor"),
            P("tensor", "dp"),
            P("tensor", "dp"),
            P(("dp", "tensor")),
        ),
        check_vma=False,
    )
```

time: 902 us -> 537 us (0.60)
  waiting for transfers between devices: 444 us -> 218 us
  blocking collectives: 189 us -> 108 us
  matrix products: 154 us -> 83.8 us
  Pallas kernels: 0 us -> 40.5 us
  local copies, waits for them, and re-layouts: 39.6 us -> 20.6 us
  other arithmetic: 53.6 us -> 34.7 us
  starting transfers between devices: 1.03 us -> 11.1 us
    all_gather x8 -> x3, waiting for transfers between devices: 212 us -> 74.5 us  [gather_weight(): lax.all_gather(shard, 'dp', axis=0, axis_index_groups=same_core, tiled=Fa...]
    unnamed x3 -> x1, blocking collectives: 145 us -> 40.2 us
    reduce_scatter x7 -> x3, waiting for transfers between devices: 151 us -> 50.2 us  [scatter_weight(): lax.psum_scatter(both, 'dp', scatter_dimension=0, axis_index_groups=same_...]
    ppermute x0 -> x14, waiting for transfers between devices: none -> 91.8 us  [the longest x4 66.5 us: scatter_rows(): lax.ppermute(product(blocks[1]).astype(BF16), 'tensor', [(0, 1), (1, 0)])]
    unnamed x17 -> x6, waiting for transfers between devices: 80.9 us -> 1.44 us
    dot_general x24 -> x20, matrix products: 154 us -> 83.8 us  [the longest x8 33.1 us: mm_t(): lax.dot_general(a, b, (((1,), (1,)), ((), ())), preferred_element_type=F32)]
    pallas_call x0 -> x2, Pallas kernels: none -> 40.5 us  [attention_call(): pl.pallas_call(kernel, grid=(group // length, width // PAIR), out_shape=[...]
    all_gather x2 -> x1, blocking collectives: 43.2 us -> 67.4 us  [local(): small = lax.all_gather(packed, ('dp', 'tensor'), axis=0, tiled=False)]
  transfers between devices with their start and end apart: 16 -> 20, of which waited for: 13 -> 10; matrix products, arithmetic and copies ran while one was open for 21% -> 23% of each run, Pallas kernels for 0% -> 8%
where the time goes in v1:
time: 537 us; the launch traced here: 531 us
  waiting for transfers between devices  218 us (41%)
  blocking collectives  108 us (20%)
  matrix products  83.8 us (16%)
  Pallas kernels  40.5 us (8%)
  other arithmetic  34.7 us (6%)
  local copies, waits for them, and re-layouts  20.6 us (4%)
  between operations  15 us (3%)
  starting transfers between devices  11.1 us (2%)
    all_gather x3, waiting for transfers between devices, gather_weight(): lax.all_gather(shard, 'dp', axis=0, axis_index_groups=same_core, tiled=Fa...  74.5 us
    all_gather x1, blocking collectives, local(): small = lax.all_gather(packed, ('dp', 'tensor'), axis=0, tiled=False)  67.4 us
    ppermute x4, waiting for transfers between devices, scatter_rows(): lax.ppermute(product(blocks[1]).astype(BF16), 'tensor', [(0, 1), (1, 0)])  66.5 us
    reduce_scatter x3, waiting for transfers between devices, scatter_weight(): lax.psum_scatter(both, 'dp', scatter_dimension=0, axis_index_groups=same_...  50.2 us
    pallas_call x2, Pallas kernels, attention_call(): pl.pallas_call(kernel, grid=(group // length, width // PAIR), out_shape=[...  40.5 us
    unnamed x1, blocking collectives  40.2 us
    dot_general x8, matrix products, mm_t(): lax.dot_general(a, b, (((1,), (1,)), ((), ())), preferred_element_type=F32)  33.1 us
    dot_general x8, matrix products, mm(): lax.dot_general(a, b, (((1,), (0,)), ((), ())), preferred_element_type=F32)  29.6 us
  transfers between devices with their start and end apart: 20, of which 10 were waited for; matrix products, arithmetic and copies ran while one was open for 23% of the time, Pallas kernels for 8%

profile of v1, /device:TPU:0, one launch (start us, length us, event | category | flops | bytes accessed | tf_op | source)
XLA Modules:
  0.0 531.3 jit_solution(12986043027060557530)
XLA Ops:
  11.4 51.4 %all-gather.9.cloned.1.call-done = bf16[512,2048]{1,0:T(8,128)(2,1)} async-done(((bf16[64,2048]{1,0:T(8,128)(2,1)}), bf16[512,2048]{1,0:T(8,128)(2,1)}) %all-gather.9.cloned.1.call-update) | async-done | bytes 2097168 | tf_op jit(solution)/shard_map/all_gather | solution.py:198
  65.3 67.4 %all-gather.4 = f32[32,1,384]{2,1,0:T(1,128)S(1)} all-gather(f32[1,1,384]{2,1,0:T(1,128)S(1)} %reshape.233), channel_id=2, replica_groups=mesh['dp'=16,'tensor'=2] {'dp','tensor'}, dimensions={0}, use_global_device_ids=true | all-gather | bytes 50688 | tf_op jit(solution)/shard_map/all_gather | solution.py:243
  139.8 23.0 %all-gather.11.cloned.1.call-done = bf16[512,2048]{1,0:T(8,128)(2,1)} async-done(((bf16[64,2048]{1,0:T(8,128)(2,1)}), bf16[512,2048]{1,0:T(8,128)(2,1)}) %all-gather.11.cloned.1.call-update) | async-done | bytes 2097168 | tf_op jit(solution)/shard_map/all_gather | solution.py:198
  162.9 2.5 select_bitcast_fusion.5
  165.8 3.8 fusion.30
  169.6 3.0 fusion.31
  173.0 14.5 %shard_map.245 = bf16[1024,512]{1,0:T(8,128)(2,1)S(1)} custom-call(s32[1]{0:T(128)} %bitcast.flip_ref, f32[8]{0:T(128)S(1)} %multiply_exponential_fusion.slope_ref, bf16[1024,512]{1,0:T(8,128)(2,1)S(1)} %get-tuple-element.107.q_ref, bf16[1024,512]{1,0:T(8,128)(2,1)S(1)} %get-tuple-element.108.k_ref, bf16[1024,512]{1,0:T(8,128)(2,1)S(1)} %get-tuple-element.106.v_ref), custom_call_target="tpu_custom_call" | custom-call | flops 4294967296 | bytes 4194304 | tf_op jit(solution)/shard_map/pallas_call | solution.py:159
  197.3 16.7 %collective-permute-done.2 = bf16[512,1024]{1,0:T(8,128)(2,1)S(1)} collective-permute-done((bf16[512,1024]{1,0:T(8,128)(2,1)S(1)}, bf16[512,1024]{1,0:T(8,128)(2,1)S(1)}, u32[]{:S(2)}, u32[]{:S(2)}) %collective-permute-start.2) | collective-permute-done | bytes 1048608 | tf_op jit(solution)/shard_map/ppermute | solution.py:222
  220.9 6.0 %fusion.6 = bf16[512,2048]{1,0:T(8,128)(2,1)S(1)} fusion(f32[512,2048]{1,0:T(8,128)S(1)} %fusion.101, bf16[512,1024]{1,0:T(8,128)(2,1)} %param.27, bf16[1024,2048]{1,0:T(8,128)(2,1)S(1)} %bitcast.160, f32[2048]{0:T(1024)S(1)} %add.195), kind=kOutput, calls=%fused_computation.11 | convolution fusion | flops 2169503744 | bytes 11542528 | tf_op jit(solution)/shard_map/dot_general | solution.py:43
  226.9 14.9 %collective-permute-done.5 = bf16[512,1024]{1,0:T(8,128)(2,1)S(1)} collective-permute-done((bf16[512,1024]{1,0:T(8,128)(2,1)S(1)}, bf16[512,1024]{1,0:T(8,128)(2,1)S(1)}, u32[]{:S(2)}, u32[]{:S(2)}) %collective-permute-start.5) | collective-permute-done | bytes 1048608 | tf_op jit(solution)/shard_map/ppermute | solution.py:217
  241.8 6.1 %multiply_convert_fusion = (bf16[512,2048]{1,0:T(8,128)(2,1)S(1)}, bf16[512,2048]{1,0:T(8,128)(2,1)}, f32[512,2048]{1,0:T(8,128)S(1)}) fusion(f32[2048]{0:T(1024)S(1)} %add.195, f32[512,2048]{1,0:T(8,128)S(1)} %fusion.101, bf16[512,1024]{1,0:T(8,128)(2,1)S(1)} %collective-permute-done.5, bf16[1024,2048]{1,0:T(8,128)(2,1)S(1)} %bitcast.165), kind=kOutput, calls=%fused_computation.44 | convolution fusion | flops 2168455168 | bytes 17833984 | tf_op jit(solution)/shard_map/dot_general | solution.py:43
  248.0 6.8 %fusion.13 = bf16[512,2048]{1,0:T(8,128)(2,1)S(1)} fusion(f32[512,2048]{1,0:T(8,128)S(1)} %get-tuple-element.137, bf16[512,1024]{1,0:T(8,128)(2,1)} %collective-permute-done.7, bf16[1024,2048]{1,0:T(8,128)(2,1)S(1)} %bitcast.161, f32[2048]{0:T(1024)S(1)} %add.195), kind=kOutput, calls=%fused_computation.18 | convolution fusion | flops 2169503744 | bytes 11542528 | tf_op jit(solution)/shard_map/dot_general | solution.py:43
  254.8 3.4 convolution_convert_fusion.3
  259.6 5.2 convolution_convert_fusion.1
  266.4 3.4 convolution_convert_fusion.4
  270.5 14.1 %collective-permute-done.8 = bf16[512,1024]{1,0:T(8,128)(2,1)} collective-permute-done((bf16[512,1024]{1,0:T(8,128)(2,1)}, bf16[512,1024]{1,0:T(8,128)(2,1)}, u32[]{:S(2)}, u32[]{:S(2)}) %collective-permute-start.8) | collective-permute-done | bytes 1048608 | tf_op jit(solution)/shard_map/ppermute | solution.py:222
  284.5 6.1 %multiply_reduce_fusion = (f32[1024]{0:T(1024)S(1)}, f32[512]{0:T(512)S(1)}, f32[512]{0:T(512)S(1)}, f32[1024]{0:T(1024)S(1)}, f32[512,1024]{1,0:T(8,128)S(1)}) fusion(f32[512,1024]{1,0:T(8,128)S(1)} %get-tuple-element.135, f32[512]{0:T(512)S(1)} %add_rsqrt_fusion, f32[512]{0:T(512)S(1)} %broadcast_multiply_fusion.4, ...), kind=kOutput, calls=%fused_computation.96 | convolution fusion | flops 2153247744 | bytes 11554816 | tf_op jit(solution)/shard_map/dot_general | solution.py:47
  290.6 14.1 %collective-permute-done.6 = bf16[512,1024]{1,0:T(8,128)(2,1)S(1)} collective-permute-done((bf16[512,1024]{1,0:T(8,128)(2,1)}, bf16[512,1024]{1,0:T(8,128)(2,1)S(1)}, u32[]{:S(2)}, u32[]{:S(2)}) %collective-permute-start.6) | collective-permute-done | bytes 1048608 | tf_op jit(solution)/shard_map/ppermute | solution.py:222
  304.7 5.6 %fusion.97 = (f32[1024]{0:T(1024)S(1)}, f32[512,1024]{1,0:T(8,128)S(1)}, bf16[512,1024]{1,0:T(8,128)(2,1)}, f32[1024]{0:T(1024)S(1)}) fusion(f32[512]{0:T(512)S(1)} %get-tuple-element.139, f32[512,1024]{1,0:T(8,128)S(1)} %get-tuple-element.135, f32[512]{0:T(512)S(1)} %broadcast_multiply_fusion.4, f32[512]{0:T(512)S(1)} %get-tuple-element.140, ...), kind=kOutput, calls=%fused_computation.181 | convolution fusion | flops 2156918784 | bytes 16801792 | tf_op jit(solution)/shard_map/dot_general | solution.py:47
  312.0 3.7 fusion.19
  316.2 7.4 %fusion.27 = bf16[1024,2048]{1,0:T(8,128)(2,1)S(1)} fusion(bf16[512,2048]{1,0:T(8,128)(2,1)} %copy-done.29, bf16[512,2048]{1,0:T(8,128)(2,1)} %get-tuple-element.133, bf16[512,1024]{1,0:T(8,128)(2,1)} %collective-permute-done.7, bf16[512,1024]{1,0:T(8,128)(2,1)} %param.27), kind=kOutput, calls=%fused_computation.46 | convolution fusion | flops 4309647360 | bytes 10485760 | tf_op jit(solution)/shard_map/dot_general | solution.py:51
  327.4 6.1 %collective-permute-done.9 = bf16[512,1024]{1,0:T(8,128)(2,1)S(1)} collective-permute-done((bf16[512,1024]{1,0:T(8,128)(2,1)S(1)}, bf16[512,1024]{1,0:T(8,128)(2,1)S(1)}, u32[]{:S(2)}, u32[]{:S(2)}) %collective-permute-start.9) | collective-permute-done | bytes 1048608 | tf_op jit(solution)/shard_map/ppermute | solution.py:217
  335.6 26.0 %shard_map.246 = (bf16[1024,512]{1,0:T(8,128)(2,1)S(1)}, bf16[1024,512]{1,0:T(8,128)(2,1)S(1)}, bf16[1024,512]{1,0:T(8,128)(2,1)S(1)}) custom-call(s32[1]{0:T(128)} %bitcast.flip_ref, f32[8]{0:T(128)S(1)} %multiply_exponential_fusion.slope_ref, bf16[1024,512]{1,0:T(8,128)(2,1)S(1)} %copy-done.2, bf16[1024,512]{1,0:T(8,128)(2,1)S(1)} %copy-done.4, ...), custom_call_target="tpu_custom_call" | custom-call | flops 10737418240 | bytes 7340032 | tf_op jit(solution)/shard_map/pallas_call | solution.py:159
  365.0 3.8 fusion.18
  371.3 6.1 %convolution_convert_fusion = bf16[1024,1536]{1,0:T(8,128)(2,1)S(1)} fusion(bf16[1024,1536]{1,0:T(8,128)(2,1)} %constant_dynamic-update-slice_fusion, bf16[512,1024]{1,0:T(8,128)(2,1)} %collective-permute-done.1, bf16[512,1024]{1,0:T(8,128)(2,1)} %fusion.39), kind=kOutput, calls=%fused_computation.47 | convolution fusion | flops 3226992640 | bytes 8388608 | tf_op jit(solution)/shard_map/dot_general | solution.py:51
  378.3 4.1 collective-permute-done.11
  384.7 5.3 fusion.73
  393.8 21.7 %collective-permute-done.10 = bf16[512,1024]{1,0:T(8,128)(2,1)} collective-permute-done((bf16[512,1024]{1,0:T(8,128)(2,1)}, bf16[512,1024]{1,0:T(8,128)(2,1)}, u32[]{:S(2)}, u32[]{:S(2)}) %collective-permute-start.10) | collective-permute-done | bytes 1048608 | tf_op jit(solution)/shard_map/ppermute | solution.py:222
  415.6 6.4 %fusion.45 = (f32[1024]{0:T(1024)S(1)}, f32[512]{0:T(512)S(1)}, f32[512]{0:T(512)S(1)}, f32[1024]{0:T(1024)S(1)}, f32[512,1024]{1,0:T(8,128)}) fusion(bf16[512,1024]{1,0:T(8,128)(2,1)S(1)} %copy-done.8, f32[512]{0:T(512)S(1)} %add_rsqrt_fusion.1, f32[512]{0:T(512)S(1)} %broadcast_multiply_fusion.5, f32[1024]{0:T(1024)S(1)} %mul.188, ...), kind=kOutput, calls=%fused_computation.75 | convolution fusion | flops 1616901120 | bytes 8933376 | tf_op jit(solution)/shard_map/dot_general | solution.py:47
  422.2 40.2 %all-reduce = f32[32,384]{1,0:T(8,128)S(1)} all-reduce(f32[32,384]{1,0:T(8,128)S(1)} %concatenate.50), channel_id=6, replica_groups=mesh['dp'=16,'tensor'=2] {'dp','tensor'}, use_global_device_ids=true, to_apply=%region_17.18.clone | all-reduce | flops 12288 | bytes 98304
  464.7 3.3 fusion.44
  471.6 50.2 %reduce-scatter.4.cloned.1.call-done = bf16[64,2048]{1,0:T(8,128)(2,1)} async-done(((bf16[512,2048]{1,0:T(8,128)(2,1)}), bf16[64,2048]{1,0:T(8,128)(2,1)}) %reduce-scatter.4.cloned.1.call-update) | async-done | bytes 262160 | tf_op jit(solution)/shard_map/reduce_scatter | solution.py:211
  (207 shorter events, 63.8 us)
Async XLA Ops:
  7.2 127.2 %copy-start.7 = (bf16[512,1024]{1,0:T(8,128)(2,1)S(1)}, bf16[512,1024]{1,0:T(8,128)(2,1)}, u32[]{:S(2)}) copy-start(bf16[512,1024]{1,0:T(8,128)(2,1)} %param.14) | copy-start | bytes 3145732
  7.2 55.6 %all-gather.9.cloned.1.call-start = ((), (), s32[]{:S(2)}) async-start(), calls=%async_computation.6 | async-start | bytes 2359296 | tf_op jit(solution)/shard_map/all_gather | solution.py:198
  9.8 129.9 %all-gather.13.cloned.1.call-start = ((), (), s32[]{:S(2)}) async-start(), calls=%async_computation.8 | async-start | bytes 2359296 | tf_op jit(solution)/shard_map/all_gather | solution.py:198
  10.6 152.3 %all-gather.11.cloned.1.call-start = ((), (), s32[]{:S(2)}) async-start(), calls=%async_computation.7 | async-start | bytes 2359296 | tf_op jit(solution)/shard_map/all_gather | solution.py:198
  11.3 456.7 %reduce-scatter.6.cloned.1.call-start = ((), (), s32[]{:S(2)}) async-start(), calls=%async_computation.4 | async-start | bytes 2359296 | tf_op jit(solution)/shard_map/reduce_scatter | solution.py:211
  62.7 100.1 %collective-permute-start = (bf16[8,64,2048]{2,1,0:T(8,128)(2,1)}, bf16[8,64,2048]{2,1,0:T(8,128)(2,1)}, u32[]{:S(2)}, u32[]{:S(2)}) collective-permute-start(bf16[8,64,2048]{2,1,0:T(8,128)(2,1)} %bitcast.172), channel_id=1, source_target_pairs={{0,2},{2,0},{4,6},{6,4},{8,10},{10,8},{12,14},{14,12},{16,18},{18,... | collective-permute-start | bytes 6291464 | tf_op jit(solution)/shard_map/ppermute | solution.py:199
  136.3 33.4 %collective-permute-start.1 = (bf16[512,1024]{1,0:T(8,128)(2,1)}, bf16[512,1024]{1,0:T(8,128)(2,1)}, u32[]{:S(2)}, u32[]{:S(2)}) collective-permute-start(bf16[512,1024]{1,0:T(8,128)(2,1)} %fusion.39), channel_id=1, source_target_pairs={{0,1},{1,0},{2,3},{3,2},{4,5},{5,4},{6,7},{7,6},{8,9},{9,8},{10,11... | collective-permute-start | bytes 3145736 | tf_op jit(solution)/shard_map/ppermute | solution.py:217
  136.3 111.7 %collective-permute-start.7 = (bf16[512,1024]{1,0:T(8,128)(2,1)}, bf16[512,1024]{1,0:T(8,128)(2,1)}, u32[]{:S(2)}, u32[]{:S(2)}) collective-permute-start(bf16[512,1024]{1,0:T(8,128)(2,1)} %param.27), channel_id=1, source_target_pairs={{0,1},{1,0},{2,3},{3,2},{4,5},{5,4},{6,7},{7,6},{8,9},{9,8},{10,11... | collective-permute-start | bytes 3145736 | tf_op jit(solution)/shard_map/ppermute | solution.py:217
  139.7 50.1 %collective-permute-start.4 = (bf16[8,64,2048]{2,1,0:T(8,128)(2,1)}, bf16[8,64,2048]{2,1,0:T(8,128)(2,1)}, u32[]{:S(2)}, u32[]{:S(2)}) collective-permute-start(bf16[8,64,2048]{2,1,0:T(8,128)(2,1)} %bitcast.170), channel_id=1, source_target_pairs={{0,2},{2,0},{4,6},{6,4},{8,10},{10,8},{12,14},{14,12},{16,18},{18,... | collective-permute-start | bytes 6291464 | tf_op jit(solution)/shard_map/ppermute | solution.py:199
  162.9 29.6 %collective-permute-start.3 = (bf16[8,64,2048]{2,1,0:T(8,128)(2,1)}, bf16[8,64,2048]{2,1,0:T(8,128)(2,1)}, u32[]{:S(2)}, u32[]{:S(2)}) collective-permute-start(bf16[8,64,2048]{2,1,0:T(8,128)(2,1)} %bitcast.168), channel_id=1, source_target_pairs={{0,2},{2,0},{4,6},{6,4},{8,10},{10,8},{12,14},{14,12},{16,18},{18,... | collective-permute-start | bytes 6291464 | tf_op jit(solution)/shard_map/ppermute | solution.py:199
  187.6 26.4 %copy-start.5 = (bf16[1024,512]{1,0:T(8,128)(2,1)}, bf16[1024,512]{1,0:T(8,128)(2,1)S(1)}, u32[]{:S(2)}) copy-start(bf16[1024,512]{1,0:T(8,128)(2,1)S(1)} %shard_map.245) | copy-start | bytes 3145732
  188.3 25.6 %collective-permute-start.2 = (bf16[512,1024]{1,0:T(8,128)(2,1)S(1)}, bf16[512,1024]{1,0:T(8,128)(2,1)S(1)}, u32[]{:S(2)}, u32[]{:S(2)}) collective-permute-start(bf16[512,1024]{1,0:T(8,128)(2,1)S(1)} %convolution_convert_fusion.2), channel_id=1, source_target_pairs={{0,1},{1,0},{2,3},{3,2},{4,5},{5,4},{6,7},{7,6},{8,9},{9,8},{10,11... | collective-permute-start | bytes 3145736 | tf_op jit(solution)/shard_map/ppermute | solution.py:222
  192.5 73.9 %copy-start.15 = (bf16[8,2,64,2048]{3,2,1,0:T(8,128)(2,1)}, bf16[8,2,64,2048]{3,2,1,0:T(8,128)(2,1)S(1)}, u32[]{:S(2)}) copy-start(bf16[8,2,64,2048]{3,2,1,0:T(8,128)(2,1)S(1)} %copy.89) | copy-start | bytes 12582916
  197.3 57.5 %copy-start.17 = (bf16[8,2,64,2048]{3,2,1,0:T(8,128)(2,1)}, bf16[8,2,64,2048]{3,2,1,0:T(8,128)(2,1)S(1)}, u32[]{:S(2)}) copy-start(bf16[8,2,64,2048]{3,2,1,0:T(8,128)(2,1)S(1)} %copy.86) | copy-start | bytes 12582916
  217.0 24.9 %collective-permute-start.5 = (bf16[512,1024]{1,0:T(8,128)(2,1)S(1)}, bf16[512,1024]{1,0:T(8,128)(2,1)S(1)}, u32[]{:S(2)}, u32[]{:S(2)}) collective-permute-start(bf16[512,1024]{1,0:T(8,128)(2,1)S(1)} %add_convert_fusion.1), channel_id=1, source_target_pairs={{0,1},{1,0},{2,3},{3,2},{4,5},{5,4},{6,7},{7,6},{8,9},{9,8},{10,11... | collective-permute-start | bytes 3145736 | tf_op jit(solution)/shard_map/ppermute | solution.py:217
  226.9 32.7 %copy-start.18 = (bf16[512,2048]{1,0:T(8,128)(2,1)}, bf16[512,2048]{1,0:T(8,128)(2,1)S(1)}, u32[]{:S(2)}) copy-start(bf16[512,2048]{1,0:T(8,128)(2,1)S(1)} %fusion.6) | copy-start | bytes 6291460
  258.1 26.4 %collective-permute-start.8 = (bf16[512,1024]{1,0:T(8,128)(2,1)}, bf16[512,1024]{1,0:T(8,128)(2,1)}, u32[]{:S(2)}, u32[]{:S(2)}) collective-permute-start(bf16[512,1024]{1,0:T(8,128)(2,1)} %convolution_convert_fusion.3), channel_id=1, source_target_pairs={{0,1},{1,0},{2,3},{3,2},{4,5},{5,4},{6,7},{7,6},{8,9},{9,8},{10,11... | collective-permute-start | bytes 3145736 | tf_op jit(solution)/shard_map/ppermute | solution.py:222
  266.4 45.6 %collective-permute-start.12 = (bf16[8,64,2048]{2,1,0:T(8,128)(2,1)}, bf16[8,64,2048]{2,1,0:T(8,128)(2,1)}, u32[]{:S(2)}, u32[]{:S(2)}) collective-permute-start(bf16[8,64,2048]{2,1,0:T(8,128)(2,1)} %dynamic-slice_bitcast_fusion.1), channel_id=1, source_target_pairs={{0,2},{2,0},{4,6},{6,4},{8,10},{10,8},{12,14},{14,12},{16,18},{18,... | collective-permute-start | bytes 6291464 | tf_op jit(solution)/shard_map/ppermute | solution.py:209
  269.8 34.9 %collective-permute-start.6 = (bf16[512,1024]{1,0:T(8,128)(2,1)}, bf16[512,1024]{1,0:T(8,128)(2,1)S(1)}, u32[]{:S(2)}, u32[]{:S(2)}) collective-permute-start(bf16[512,1024]{1,0:T(8,128)(2,1)} %convolution_convert_fusion.4), channel_id=1, source_target_pairs={{0,1},{1,0},{2,3},{3,2},{4,5},{5,4},{6,7},{7,6},{8,9},{9,8},{10,11... | collective-permute-start | bytes 3145736 | tf_op jit(solution)/shard_map/ppermute | solution.py:222
  270.5 34.2 %copy-start.16 = (bf16[8,2,64,2048]{3,2,1,0:T(8,128)(2,1)S(1)}, bf16[8,2,64,2048]{3,2,1,0:T(8,128)(2,1)}, u32[]{:S(2)}) copy-start(bf16[8,2,64,2048]{3,2,1,0:T(8,128)(2,1)} %copy-done.15) | copy-start | bytes 12582916
  270.5 34.2 %copy-start.30 = (bf16[512,2048]{1,0:T(8,128)(2,1)S(1)}, bf16[512,2048]{1,0:T(8,128)(2,1)}, u32[]{:S(2)}) copy-start(bf16[512,2048]{1,0:T(8,128)(2,1)} %get-tuple-element.133) | copy-start | bytes 6291460
  310.5 23.0 %collective-permute-start.9 = (bf16[512,1024]{1,0:T(8,128)(2,1)S(1)}, bf16[512,1024]{1,0:T(8,128)(2,1)S(1)}, u32[]{:S(2)}, u32[]{:S(2)}) collective-permute-start(bf16[512,1024]{1,0:T(8,128)(2,1)S(1)} %convert_element_type.156), channel_id=1, source_target_pairs={{0,1},{1,0},{2,3},{3,2},{4,5},{5,4},{6,7},{7,6},{8,9},{9,8},{10,11... | collective-permute-start | bytes 3145736 | tf_op jit(solution)/shard_map/ppermute | solution.py:217
  315.7 154.1 %reduce-scatter.8.cloned.1.call-start = ((), (), s32[]{:S(2)}) async-start(), calls=%async_computation.5 | async-start | bytes 2359296 | tf_op jit(solution)/shard_map/reduce_scatter | solution.py:211
  325.2 39.8 %collective-permute-start.13 = (bf16[8,64,2048]{2,1,0:T(8,128)(2,1)}, bf16[8,64,2048]{2,1,0:T(8,128)(2,1)}, u32[]{:S(2)}, u32[]{:S(2)}) collective-permute-start(bf16[8,64,2048]{2,1,0:T(8,128)(2,1)} %dynamic-slice_bitcast_fusion), channel_id=1, source_target_pairs={{0,2},{2,0},{4,6},{6,4},{8,10},{10,8},{12,14},{14,12},{16,18},{18,... | collective-permute-start | bytes 6291464 | tf_op jit(solution)/shard_map/ppermute | solution.py:209
  335.6 27.1 %copy-start.6 = (bf16[1024,512]{1,0:T(8,128)(2,1)S(1)}, bf16[1024,512]{1,0:T(8,128)(2,1)}, u32[]{:S(2)}) copy-start(bf16[1024,512]{1,0:T(8,128)(2,1)} %copy-done.5) | copy-start | bytes 3145732
  335.6 27.1 %copy-start.25 = (bf16[512,1024]{1,0:T(8,128)(2,1)S(1)}, bf16[512,1024]{1,0:T(8,128)(2,1)}, u32[]{:S(2)}) copy-start(bf16[512,1024]{1,0:T(8,128)(2,1)} %copy-done.24) | copy-start | bytes 3145732
  335.6 27.1 %copy-start.28 = (bf16[512,1024]{1,0:T(8,128)(2,1)S(1)}, bf16[512,1024]{1,0:T(8,128)(2,1)}, u32[]{:S(2)}) copy-start(bf16[512,1024]{1,0:T(8,128)(2,1)} %copy-done.27) | copy-start | bytes 3145732
  368.8 152.9 %reduce-scatter.4.cloned.1.call-start = ((), (), s32[]{:S(2)}) async-start(), calls=%async_computation.3 | async-start | bytes 2359296 | tf_op jit(solution)/shard_map/reduce_scatter | solution.py:211
  378.2 4.2 collective-permute-start.11
  390.0 25.5 %copy-start.8 = (bf16[512,1024]{1,0:T(8,128)(2,1)S(1)}, bf16[512,1024]{1,0:T(8,128)(2,1)}, u32[]{:S(2)}) copy-start(bf16[512,1024]{1,0:T(8,128)(2,1)} %param.14) | copy-start | bytes 3145732
  390.0 25.5 %collective-permute-start.10 = (bf16[512,1024]{1,0:T(8,128)(2,1)}, bf16[512,1024]{1,0:T(8,128)(2,1)}, u32[]{:S(2)}, u32[]{:S(2)}) collective-permute-start(bf16[512,1024]{1,0:T(8,128)(2,1)} %fusion.73), channel_id=1, source_target_pairs={{0,1},{1,0},{2,3},{3,2},{4,5},{5,4},{6,7},{7,6},{8,9},{9,8},{10,11... | collective-permute-start | bytes 3145736 | tf_op jit(solution)/shard_map/ppermute | solution.py:222
  393.8 70.9 %copy-start.10 = (f32[512,1024]{1,0:T(8,128)S(1)}, f32[512,1024]{1,0:T(8,128)}, u32[]{:S(2)}) copy-start(f32[512,1024]{1,0:T(8,128)} %copy-done.9) | copy-start | bytes 6291460
  (19 other events, 165.7 us)
Sparse Core Ops, SparseCore 0:
  10.7 51.9 all-gather.8
  64.9 47.8 all-gather.12
  114.9 47.9 all-gather.10
  315.8 65.4 reduce-scatter.5
  384.7 67.0 reduce-scatter.7
  455.3 66.4 reduce-scatter.3

commit v2 on v1

--- a/solution.py
+++ b/solution.py
@@ -168,6 +168,315 @@
     )(flip, slopes, *operands)
 
 
+def ring_place(chip, chips):
+    return chip // 2 + (chip % 2) * (chips - 1 - 2 * (chip // 2))
+
+
+def ring_chip(place, chips):
+    place = lax.rem(place + 2 * chips, chips)
+    far = place // (chips // 2)
+    return far * (2 * (chips - 1 - place) + 1) + (1 - far) * 2 * place
+
+
+def remote(src, dst, send, recv, device):
+    return pltpu.make_async_remote_copy(
+        src_ref=src,
+        dst_ref=dst,
+        send_sem=send,
+        recv_sem=recv,
+        device_id=device,
+        device_id_type=pl.DeviceIdType.MESH,
+    )
+
+
+def greet(devices):
+    barrier = pltpu.get_barrier_semaphore()
+    for device in devices:
+        pl.semaphore_signal(barrier, inc=1, device_id=device, device_id_type=pl.DeviceIdType.MESH)
+    pl.semaphore_wait(barrier, len(devices))
+
+
+def neighbours(chips, parts):
+    index = lax.axis_index("dp")
+    tensor = lax.axis_index("tensor")
+    core = lax.rem(index, 2)
+    place = ring_place(index // 2, chips)
+    right = (ring_chip(place + 1, chips) * 2 + core, tensor)
+    left = (ring_chip(place - 1, chips) * 2 + core, tensor)
+    twin = (index + 1 - 2 * core, tensor)
+    peers = [(index, lax.rem(tensor + k, parts)) for k in range(1, parts)]
+    return core, place, tensor, right, left, twin, peers
+
+
+def gather_kernel(chips, parts, *refs):
+    pair = parts == 2
+    if pair:
+        x_ref, small_ref, tok_ref, full_ref, all_ref, other_ref = refs[:6]
+        sems = refs[6:]
+    else:
+        x_ref, small_ref, full_ref, all_ref = refs[:4]
+        sems = refs[4:]
+    here_sem, big_s, big_r, swap_s, swap_r, sm_s, sm_r, smw_s, smw_r, ten_s, ten_r, tok_s, tok_r = sems
+    core, place, tensor, right, left, twin, peers = neighbours(chips, parts)
+    mine = ring_chip(place, chips)
+    steps = chips // 2
+    half = x_ref.shape[0] // 2
+    greet([right, left, twin] + peers)
+    waits = []
+    if pair:
+        tok = remote(tok_ref, other_ref, tok_s.at[0], tok_r.at[0], peers[0])
+        tok.start()
+    here = pltpu.make_async_copy(x_ref, full_ref.at[mine, core], here_sem.at[0])
+    here.start()
+    here_small = pltpu.make_async_copy(small_ref, all_ref.at[tensor, mine, core], here_sem.at[1])
+    here_small.start()
+    swaps = []
+    small_swaps = []
+
+    def swap(chip, first):
+        n = len(swaps)
+        small_src = small_ref if first else all_ref.at[tensor, chip, core]
+        copy = remote(small_src, all_ref.at[tensor, chip, core], smw_s.at[n], smw_r.at[n], twin)
+        copy.start()
+        small_swaps.append(copy)
+        src = x_ref if first else full_ref.at[chip, core]
+        copy = remote(src, full_ref.at[chip, core], swap_s.at[n], swap_r.at[n], twin)
+        copy.start()
+        swaps.append(copy)
+
+    previous = []
+    for step in range(steps):
+        started = []
+        for copy in previous:
+            copy.wait_recv()
+        for side, device in ((0, right), (1, left)):
+            chip = ring_chip(place - step if side == 0 else place + step, chips)
+            slot = side * steps + step
+            if step < steps - 1 or side == 0:
+                src = small_ref if step == 0 else all_ref.at[tensor, chip, core]
+                copy = remote(
+                    src, all_ref.at[tensor, chip, core], sm_s.at[slot], sm_r.at[slot], device
+                )
+                copy.start()
+                started.append(copy)
+            src = x_ref if step == 0 else full_ref.at[chip, core]
+            dst = full_ref.at[chip, core]
+            if step == steps - 1:
+                rows = pl.ds(side * half, half)
+                src, dst = src.at[rows], dst.at[rows]
+            copy = remote(src, dst, big_s.at[slot], big_r.at[slot], device)
+            copy.start()
+            started.append(copy)
+        if step == 0:
+            swap(mine, True)
+        else:
+            swap(ring_chip(place - step, chips), False)
+            swap(ring_chip(place + step, chips), False)
+        waits += started
+        previous = started
+    for copy in previous:
+        copy.wait_recv()
+    swap(ring_chip(place + steps, chips), False)
+    here_small.wait()
+    for copy in small_swaps:
+        copy.wait_recv()
+    spread = []
+    for k, peer in enumerate(peers):
+        copy = remote(all_ref.at[tensor], all_ref.at[tensor], ten_s.at[k], ten_r.at[k], peer)
+        copy.start()
+        spread.append(copy)
+    here.wait()
+    for copy in swaps:
+        copy.wait_recv()
+    for copy in waits + swaps + small_swaps:
+        copy.wait_send()
+    for copy in spread:
+        copy.wait()
+    if pair:
+        tok.wait()
+
+
+def gather_call(shard, small, tokens, chips, parts):
+    rows, columns = shard.shape
+    anywhere = pl.BlockSpec(memory_space=pl.ANY)
+    out = [
+        jax.ShapeDtypeStruct((chips, 2, rows, columns), BF16),
+        jax.ShapeDtypeStruct((parts, chips, 2) + small.shape, F32),
+    ]
+    operands = [shard, small]
+    if parts == 2:
+        out.append(jax.ShapeDtypeStruct(tokens.shape, BF16))
+        operands.append(tokens)
+    sem = pltpu.SemaphoreType.DMA
+    result = pl.pallas_call(
+        functools.partial(gather_kernel, chips, parts),
+        out_shape=out,
+        in_specs=[anywhere] * len(operands),
+        out_specs=[anywhere] * len(out),
+        scratch_shapes=[sem((2,))]
+        + [sem((chips,))] * 8
+        + [sem((parts - 1,))] * 2
+        + [sem((1,))] * 2,
+        compiler_params=pltpu.CompilerParams(collective_id=0, has_side_effects=True),
+        cost_estimate=pl.CostEstimate(
+            flops=0, bytes_accessed=64 * rows * columns, transcendentals=0
+        ),
+    )(*operands)
+    return list(result) + [None] * (3 - len(out))
+
+
+def reduce_kernel(chips, parts, g_ref, s_ref, o_ref, so_ref, *scratch):
+    (pair_in, ring_in, ring_out, sm_ten, sm_sum, sm_pair, sm_in, sm_out) = scratch[:8]
+    pair_s, pair_r, big_s, big_r, ten_s, ten_r, smp_s, smp_r, sm_s, sm_r = scratch[8:]
+    core, place, tensor, right, left, twin, peers = neighbours(chips, parts)
+    steps = chips // 2
+    half = g_ref.shape[2] // 2
+    greet([right, left, twin] + peers)
+    order = [steps]
+    for n in reversed(range(1, steps)):
+        order += [-n, n]
+    order.append(0)
+    away = 1 - core
+    done = []
+    ten = []
+    for k, peer in enumerate(peers):
+        goal = lax.rem(tensor + k + 1, parts)
+        copy = remote(s_ref.at[goal], sm_ten.at[k], ten_s.at[k], ten_r.at[k], peer)
+        copy.start()
+        ten.append(copy)
+    pairs = {}
+    for n, shift in enumerate(order):
+        chip = ring_chip(place + shift, chips)
+        copy = remote(g_ref.at[chip, away], pair_in.at[n], pair_s.at[n], pair_r.at[n], twin)
+        copy.start()
+        pairs[shift] = (n, copy)
+
+    def own(shift):
+        n, copy = pairs[shift]
+        if shift not in done:
+            copy.wait_recv()
+            done.append(shift)
+        chip = ring_chip(place + shift, chips)
+        return g_ref[chip, core].astype(F32) + pair_in[n].astype(F32)
+
+    for copy in ten:
+        copy.wait_recv()
+    total = s_ref[tensor]
+    for k in range(len(peers)):
+        total = total + sm_ten[k]
+    sm_sum[...] = total
+    sm_pair_copy = remote(sm_sum.at[away], sm_pair, smp_s.at[0], smp_r.at[0], twin)
+    sm_pair_copy.start()
+    sends = list(ten)
+    arrived = {}
+    for step in range(steps):
+        for side, device in ((0, left), (1, right)):
+            shift = (step - steps) if side == 0 else (steps - step)
+            slot = side * steps + step
+            if step == 0:
+                rows = pl.ds(side * half, half)
+                ring_out[slot] = own(steps).astype(BF16)
+                copy = remote(
+                    ring_out.at[slot, rows],
+                    ring_in.at[slot, rows],
+                    big_s.at[slot],
+                    big_r.at[slot],
+                    device,
+                )
+            else:
+                value = own(shift)
+                arrived[side].wait_recv()
+                if step == 1:
+                    rows = slice(side * half, (side + 1) * half)
+                    rest = slice((1 - side) * half, (2 - side) * half)
+                    ring_out[slot, rows] = (
+                        value[rows] + ring_in[slot - 1, rows].astype(F32)
+                    ).astype(BF16)
+                    ring_out[slot, rest] = value[rest].astype(BF16)
+                else:
+                    ring_out[slot] = (value + ring_in[slot - 1].astype(F32)).astype(BF16)
+                copy = remote(
+                    ring_out.at[slot], ring_in.at[slot], big_s.at[slot], big_r.at[slot], device
+                )
+            copy.start()
+            arrived[side] = copy
+            sends.append(copy)
+    sm_pair_copy.wait_recv()
+    kept = {}
+    small_arrived = {}
+
+    def own_small(shift):
+        chip = ring_chip(place + shift, chips)
+        return sm_sum[core, chip] + sm_pair[chip]
+
+    for step in range(steps):
+        for side, device in ((0, left), (1, right)):
+            if step == 0 and side == 1:
+                continue
+            shift = (step - steps) if side == 0 else (steps - step)
+            slot = side * steps + step
+            value = own_small(shift)
+            if side in small_arrived:
+                small_arrived[side].wait_recv()
+                value = value + sm_in[slot - 1]
+            sm_out[slot] = value
+            copy = remote(sm_out.at[slot], sm_in.at[slot], sm_s.at[slot], sm_r.at[slot], device)
+            copy.start()
+            small_arrived[side] = copy
+            sends.append(copy)
+    value = own(0)
+    for side in range(2):
+        arrived[side].wait_recv()
+        value = value + ring_in[(side + 1) * steps - 1].astype(F32)
+    o_ref[...] = value
+    value = own_small(0)
+    for side in range(2):
+        small_arrived[side].wait_recv()
+        value = value + sm_in[(side + 1) * steps - 1]
+    so_ref[...] = value
+    for _, copy in pairs.values():
+        copy.wait_send()
+    sm_pair_copy.wait_send()
+    for copy in sends:
+        copy.wait_send()
+
+
+def reduce_call(grad, small, chips, parts):
+    rows, columns = grad.shape[2:]
+    tile = small.shape[3:]
+    sem = pltpu.SemaphoreType.DMA
+    vmem = pl.BlockSpec(memory_space=pltpu.VMEM)
+    return pl.pallas_call(
+        functools.partial(reduce_kernel, chips, parts),
+        out_shape=[
+            jax.ShapeDtypeStruct((rows, columns), F32),
+            jax.ShapeDtypeStruct(tile, F32),
+        ],
+        in_specs=[vmem, vmem],
+        out_specs=[vmem, vmem],
+        scratch_shapes=[
+            pltpu.VMEM((chips, rows, columns), BF16),
+            pltpu.VMEM((chips, rows, columns), BF16),
+            pltpu.VMEM((chips, rows, columns), BF16),
+            pltpu.VMEM((parts - 1, 2, chips) + tile, F32),
+            pltpu.VMEM((2, chips) + tile, F32),
+            pltpu.VMEM((chips,) + tile, F32),
+            pltpu.VMEM((chips,) + tile, F32),
+            pltpu.VMEM((chips,) + tile, F32),
+        ]
+        + [sem((chips,))] * 4
+        + [sem((parts - 1,))] * 2
+        + [sem((1,))] * 2
+        + [sem((chips,))] * 2,
+        compiler_params=pltpu.CompilerParams(
+            collective_id=1, has_side_effects=True, vmem_limit_bytes=40 * 1024 * 1024
+        ),
+        cost_estimate=pl.CostEstimate(
+            flops=0, bytes_accessed=64 * rows * columns, transcendentals=0
+        ),
+    )(grad, small)
+
+
 def local(
     tokens,
     gain_one,
@@ -188,29 +497,13 @@
     n_dp = lax.axis_size("dp")
     everyone = n_dp * parts
     t_index = lax.axis_index("tensor")
-    core = lax.axis_index("dp") % 2
     chips = n_dp // 2
-    swap_cores = [(i, i ^ 1) for i in range(n_dp)]
-    same_core = [list(range(c, n_dp, 2)) for c in range(2)]
 
     def gather_weight(shard):
-        rows, columns = shard.shape
-        mine = lax.all_gather(shard, "dp", axis=0, axis_index_groups=same_core, tiled=False)
-        theirs = lax.ppermute(mine, "dp", swap_cores)
-        first = jnp.where(core == 0, mine, theirs)
-        second = jnp.where(core == 0, theirs, mine)
-        return jnp.stack([first, second], axis=1).reshape(n_dp * rows, columns)
+        return lax.all_gather(shard, "dp", axis=0, tiled=True)
 
     def scatter_weight(grad):
-        rows, columns = grad.shape
-        blocks = grad.reshape(chips, 2, rows // n_dp, columns)
-        away = lax.dynamic_index_in_dim(blocks, 1 - core, 1, keepdims=False).astype(BF16)
-        keep = lax.dynamic_index_in_dim(blocks, core, 1, keepdims=False).astype(F32)
-        both = (keep + lax.ppermute(away, "dp", swap_cores).astype(F32)).astype(BF16)
-        both = both.reshape(rows // 2, columns)
-        return lax.psum_scatter(
-            both, "dp", scatter_dimension=0, axis_index_groups=same_core, tiled=True
-        ).astype(F32)
+        return lax.psum_scatter(grad, "dp", scatter_dimension=0, tiled=True).astype(F32)
 
     def gather_rows(mine):
         if parts == 2:
@@ -240,11 +533,19 @@
         [gain_one, shift_one, bias_out, gain_two, shift_two, bias_down]
         + [bias_qv.astype(F32).reshape(-1), bias_up.astype(F32).reshape(-1)]
     )
-    small = lax.all_gather(packed, ("dp", "tensor"), axis=0, tiled=False)
+    tile = (8, 128)
+    pad = tile[0] * tile[1] - packed.size
+    first_shard = jnp.concatenate([w_qkv[0], w_qkv[1], w_qkv[2], w_out.T], axis=1)
+    first_full, small, other_tokens = gather_call(
+        first_shard, jnp.pad(packed, (0, pad)).reshape(tile), tokens, chips, parts
+    )
+    first_full = first_full.reshape(-1, first_shard.shape[1])
+    small = small.reshape(parts, n_dp, -1).transpose(1, 0, 2).reshape(everyone, -1)
     gain_a, shift_a, out_shift, gain_b, shift_b, down_shift = (
         small[:, n * vec : (n + 1) * vec].reshape(-1) for n in range(6)
     )
     at = 6 * vec
+    end = at + n_qv + n_bu
     local_small = lax.dynamic_index_in_dim(
         small.reshape(n_dp, parts, -1), t_index, 1, keepdims=False
     )
@@ -257,16 +558,13 @@
         .reshape(2, width)
     )
     up_shift = (
-        local_small[:, at + n_qv :]
+        local_small[:, at + n_qv : end]
         .reshape(n_dp, bias_up.shape[0], -1)
         .transpose(1, 0, 2)
         .reshape(-1)
     )
     hidden_units = up_shift.shape[0]
 
-    first_full = gather_weight(
-        jnp.concatenate([w_qkv[0], w_qkv[1], w_qkv[2], w_out.T], axis=1)
-    )
     up_full = gather_weight(w_up)
     down_t = gather_weight(w_down.T)
     qkv_full = first_full[:, : 3 * width]
@@ -283,7 +581,12 @@
     cot_blocks = gather_rows(cotangent)
     inputs = tokens.astype(F32)
     normed_one, inverse_one = normalize(inputs)
-    one_blocks = gather_rows((normed_one * gain_a + shift_a).astype(BF16))
+    low_one = (normed_one * gain_a + shift_a).astype(BF16)
+    if parts == 2:
+        other_normed = normalize(other_tokens.astype(F32))[0]
+        one_blocks = [low_one, (other_normed * gain_a + shift_a).astype(BF16)]
+    else:
+        one_blocks = gather_rows(low_one)
     qkv_shift = jnp.concatenate([qv_shift[0], jnp.zeros((width,), F32), qv_shift[1]])
     qkv_low = joined([(mm(b, qkv_full) + qkv_shift).astype(BF16) for b in one_blocks])
     query, keys, values = (qkv_low[:, n * width : (n + 1) * width] for n in range(3))
@@ -353,7 +656,6 @@
         ],
         axis=1,
     )
-    summed_first = scatter_weight(grad_first)
     grad_qv_shift = jnp.stack(
         [
             jnp.sum(grad_qkv_parts[0].astype(F32), axis=0),
@@ -387,9 +689,15 @@
         ],
         axis=1,
     )
-    sums = lax.psum_scatter(
-        packed_grads, ("dp", "tensor"), scatter_dimension=0, tiled=True
-    ).reshape(-1)
+    packed_grads = (
+        jnp.pad(packed_grads, ((0, 0), (0, pad)))
+        .reshape((chips, 2, parts) + tile)
+        .transpose(2, 1, 0, 3, 4)
+    )
+    summed_first, sums = reduce_call(
+        grad_first.reshape(chips, 2, -1, grad_first.shape[1]), packed_grads, chips, parts
+    )
+    sums = sums.reshape(-1)
     sum_gain_a, sum_shift_a, sum_out_shift, sum_gain_b, sum_shift_b, sum_down_shift = (
         sums[n * vec : (n + 1) * vec] for n in range(6)
     )
@@ -406,7 +714,7 @@
         sum_gain_b,
         sum_shift_b,
         summed_up,
-        sums[at + n_qv :].reshape(bias_up.shape),
+        sums[at + n_qv : end].reshape(bias_up.shape),
         summed_down.T,
         sum_down_shift,
     )

time: 537 us -> 403 us (0.75)
  blocking collectives: 108 us -> 0 us
  waiting for transfers between devices: 218 us -> 114 us
  Pallas kernels: 40.5 us -> 136 us
  other arithmetic: 34.7 us -> 19.8 us
  starting transfers between devices: 11.1 us -> 5.41 us
    pallas_call x0 -> x2, Pallas kernels: none -> 95.5 us  [the longest x1 52.4 us: gather_call(): pl.pallas_call(functools.partial(gather_kernel, chips, parts), out_shape=...]
    all_gather x3 -> x2, waiting for transfers between devices: 74.5 us -> 0.01 us  [gather_weight(): return lax.all_gather(shard, 'dp', axis=0, tiled=True)]
    all_gather x1 -> x0, blocking collectives: 67.4 us -> none  [local(): small = lax.all_gather(packed, ('dp', 'tensor'), axis=0, tiled=False)]
    reduce_scatter x3 -> x2, waiting for transfers between devices: 50.2 us -> 0.01 us  [scatter_weight(): lax.psum_scatter(grad, 'dp', scatter_dimension=0, tiled=True).astype(F32)]
    unnamed x1 -> x0, blocking collectives: 40.2 us -> none
    ppermute x4 -> x3, waiting for transfers between devices: 21.1 us -> 40 us  [gather_rows(): return [mine, lax.ppermute(mine, 'tensor', [(0, 1), (1, 0)])]]
    convert_element_type x6 -> x2, other arithmetic: 13.7 us -> 2.6 us  [the longest x1 1.78 us: scatter_weight(): lax.psum_scatter(grad, 'dp', scatter_dimension=0, tiled=True).astype(F32)]
    another operation x6 -> x0, other arithmetic: 7.39 us -> none  [gather_weight(): return jnp.stack([first, second], axis=1).reshape(n_dp * rows, columns)]
  transfers between devices with their start and end apart: 20 -> 11, of which waited for: 10 -> 6; matrix products, arithmetic and copies ran while one was open for 23% -> 24% of each run, Pallas kernels for 8% -> 34%
where the time goes in v2:
time: 403 us; the launch traced here: 398 us
  Pallas kernels  136 us (34%)
  waiting for transfers between devices  114 us (28%)
  matrix products  84.6 us (21%)
  local copies, waits for them, and re-layouts  22.7 us (6%)
  other arithmetic  19.8 us (5%)
  between operations  14.9 us (4%)
  starting transfers between devices  5.41 us (1%)
    ppermute x4, waiting for transfers between devices, scatter_rows(): lax.ppermute(product(blocks[1]).astype(BF16), 'tensor', [(0, 1), (1, 0)])  73 us
    pallas_call x1, Pallas kernels, gather_call(): pl.pallas_call(functools.partial(gather_kernel, chips, parts), out_shape=...  52.4 us
    pallas_call x1, Pallas kernels, reduce_call(): pl.pallas_call(functools.partial(reduce_kernel, chips, parts), out_shape=...  43.1 us
    pallas_call x2, Pallas kernels, attention_call(): pl.pallas_call(kernel, grid=(group // length, width // PAIR), out_shape=[...  40.7 us
    ppermute x3, waiting for transfers between devices, gather_rows(): return [mine, lax.ppermute(mine, 'tensor', [(0, 1), (1, 0)])]  40 us
    dot_general x8, matrix products, mm(): lax.dot_general(a, b, (((1,), (0,)), ((), ())), preferred_element_type=F32)  32.7 us
    dot_general x8, matrix products, mm_t(): lax.dot_general(a, b, (((1,), (1,)), ((), ())), preferred_element_type=F32)  31.5 us
    dot_general x4, matrix products, t_mm(): lax.dot_general(a, b, (((0,), (0,)), ((), ())), preferred_element_type=F32)  20.4 us
  transfers between devices with their start and end apart: 11, of which 6 were waited for; matrix products, arithmetic and copies ran while one was open for 24% of the time, Pallas kernels for 34%

profile of v2, /device:TPU:0, one launch (start us, length us, event | category | flops | bytes accessed | tf_op | source)
XLA Modules:
  0.0 397.9 jit_solution(18054985766977110470)
XLA Ops:
  14.4 52.4 %shard_map.245 = (bf16[8,2,64,2048]{3,2,1,0:T(8,128)(2,1)}, f32[2,8,2,8,128]{4,3,2,1,0:T(8,128)}, bf16[512,1024]{1,0:T(8,128)(2,1)}) custom-call(bf16[64,2048]{1,0:T(8,128)(2,1)} %pad_maximum_fusion.6.refs_0_, f32[8,128]{1,0:T(8,128)} %pad_bitcast_fusion.1.refs_1_, bf16[512,1024]{1,0:T(8,128)(2,1)} %refs_2_.1), custom_call_target="tpu_custom_call" | custom-call | bytes 8388608 | tf_op jit(solution)/shard_map/pallas_call | solution.py:311
  71.2 2.1 copy-done.25
  77.2 14.8 %shard_map.246 = bf16[1024,512]{1,0:T(8,128)(2,1)S(1)} custom-call(s32[1]{0:T(128)} %bitcast.flip_ref, f32[8]{0:T(128)S(1)} %multiply_exponential_fusion.slope_ref, bf16[1024,512]{1,0:T(8,128)(2,1)S(1)} %get-tuple-element.87.q_ref, bf16[1024,512]{1,0:T(8,128)(2,1)S(1)} %get-tuple-element.88.k_ref, bf16[1024,512]{1,0:T(8,128)(2,1)S(1)} %get-tuple-element.86.v_ref), custom_call_target="tpu_custom_call" | custom-call | flops 4294967296 | bytes 4194304 | tf_op jit(solution)/shard_map/pallas_call | solution.py:159
  96.3 23.9 %collective-permute-done = bf16[512,1024]{1,0:T(8,128)(2,1)} collective-permute-done((bf16[512,1024]{1,0:T(8,128)(2,1)}, bf16[512,1024]{1,0:T(8,128)(2,1)}, u32[]{:S(2)}, u32[]{:S(2)}) %collective-permute-start) | collective-permute-done | bytes 1048608 | tf_op jit(solution)/shard_map/ppermute | solution.py:515
  120.1 2.6 fusion.98
  124.2 7.1 %fusion.101 = f32[512,2048]{1,0:T(8,128)} fusion(bf16[512,1024]{1,0:T(8,128)(2,1)} %param.27, bf16[1024,2048]{1,0:T(8,128)(2,1)} %all-gather.5.cloned.1.call-done), kind=kOutput, calls=%fused_computation.166 | convolution fusion | flops 2147483648 | bytes 9437184 | tf_op jit(solution)/shard_map/dot_general | solution.py:43
  131.3 4.7 %fusion.99 = f32[512,2048]{1,0:T(8,128)S(1)} fusion(bf16[512,1024]{1,0:T(8,128)(2,1)S(1)} %add_convert_fusion.1, bf16[1024,2048]{1,0:T(8,128)(2,1)} %all-gather.3.cloned.1.call-done), kind=kOutput, calls=%fused_computation.164 | convolution fusion | flops 2147483648 | bytes 9437184 | tf_op jit(solution)/shard_map/dot_general | solution.py:43
  136.0 28.7 %collective-permute-done.1 = bf16[512,1024]{1,0:T(8,128)(2,1)S(1)} collective-permute-done((bf16[512,1024]{1,0:T(8,128)(2,1)S(1)}, bf16[512,1024]{1,0:T(8,128)(2,1)S(1)}, u32[]{:S(2)}, u32[]{:S(2)}) %collective-permute-start.1) | collective-permute-done | bytes 1048608 | tf_op jit(solution)/shard_map/ppermute | solution.py:510
  164.7 2.4 fusion.100
  167.1 10.6 %fusion.13 = (bf16[512,2048]{1,0:T(8,128)(2,1)S(1)}, bf16[512,2048]{1,0:T(8,128)(2,1)S(1)}, bf16[512,2048]{1,0:T(8,128)(2,1)S(1)}, bf16[512,2048]{1,0:T(8,128)(2,1)}) fusion(f32[512,2048]{1,0:T(8,128)S(1)} %fusion.100, f32[2048]{0:T(1024)S(1)} %add.185, f32[512,2048]{1,0:T(8,128)S(1)} %fusion.99, f32[512,2048]{1,0:T(8,128)S(1)} %copy-done.33, ...), kind=kOutput, calls=%fused_computation.18 | convolution fusion | flops 2195718144 | bytes 26222592 | tf_op jit(solution)/shard_map/dot_general | solution.py:43
  179.8 7.7 %fusion.18 = bf16[1024,2048]{1,0:T(8,128)(2,1)} fusion(bf16[512,2048]{1,0:T(8,128)(2,1)S(1)} %get-tuple-element.83, bf16[512,2048]{1,0:T(8,128)(2,1)S(1)} %get-tuple-element.106, bf16[512,1024]{1,0:T(8,128)(2,1)} %collective-permute-done.3, bf16[512,1024]{1,0:T(8,128)(2,1)} %param.27), kind=kOutput, calls=%fused_computation.27 | convolution fusion | flops 4309647360 | bytes 10485760 | tf_op jit(solution)/shard_map/dot_general | solution.py:51
  187.6 5.8 %convolution_convert_fusion.3 = bf16[512,1024]{1,0:T(8,128)(2,1)} fusion(bf16[512,2048]{1,0:T(8,128)(2,1)S(1)} %get-tuple-element.82, bf16[1024,2048]{1,0:T(8,128)(2,1)} %all-gather.3.cloned.1.call-done), kind=kOutput, calls=%fused_computation.103 | convolution fusion | flops 2148007936 | bytes 7340032 | tf_op jit(solution)/shard_map/dot_general | solution.py:47
  193.7 3.3 convolution_convert_fusion.4
  198.9 20.8 %collective-permute-done.4 = bf16[512,1024]{1,0:T(8,128)(2,1)} collective-permute-done((bf16[512,1024]{1,0:T(8,128)(2,1)}, bf16[512,1024]{1,0:T(8,128)(2,1)}, u32[]{:S(2)}, u32[]{:S(2)}) %collective-permute-start.4) | collective-permute-done | bytes 1048608 | tf_op jit(solution)/shard_map/ppermute | solution.py:515
  219.8 6.5 %multiply_reduce_fusion = (f32[1024]{0:T(1024)S(1)}, f32[512]{0:T(512)S(1)}, f32[512]{0:T(512)S(1)}, f32[1024]{0:T(1024)S(1)}, f32[512,1024]{1,0:T(8,128)S(1)}) fusion(f32[512,1024]{1,0:T(8,128)S(1)} %copy-done.13, f32[512]{0:T(512)S(1)} %add_rsqrt_fusion, f32[512]{0:T(512)S(1)} %broadcast_multiply_fusion.4, bf16[512,1024]{1,0:T(8,128)(2,1)} %collective-permute-done.4, ...), kind=kOutput, calls=%fused_computation.82 | convolution fusion | flops 2153247744 | bytes 11554816 | tf_op jit(solution)/shard_map/dot_general | solution.py:47
  226.3 14.8 %collective-permute-done.2 = bf16[512,1024]{1,0:T(8,128)(2,1)} collective-permute-done((bf16[512,1024]{1,0:T(8,128)(2,1)}, bf16[512,1024]{1,0:T(8,128)(2,1)}, u32[]{:S(2)}, u32[]{:S(2)}) %collective-permute-start.2) | collective-permute-done | bytes 1048608 | tf_op jit(solution)/shard_map/ppermute | solution.py:515
  241.1 6.0 %fusion.94 = (f32[1024]{0:T(1024)S(1)}, f32[512,1024]{1,0:T(8,128)S(1)}, bf16[512,1024]{1,0:T(8,128)(2,1)}, f32[1024]{0:T(1024)S(1)}) fusion(f32[512]{0:T(512)S(1)} %get-tuple-element.120, f32[512,1024]{1,0:T(8,128)S(1)} %copy-done.13, f32[512]{0:T(512)S(1)} %broadcast_multiply_fusion.4, f32[512]{0:T(512)S(1)} %get-tuple-element.121, f32[1024]{0:T(1024)S(1)} %mul.215, ...), kind=kOutput, calls=%fused_computation.159 | convolution fusion | flops 2156918784 | bytes 16801792 | tf_op jit(solution)/shard_map/dot_general | solution.py:47
  250.2 6.3 %convolution_convert_fusion.1 = bf16[1024,2048]{1,0:T(8,128)(2,1)} fusion(bf16[512,2048]{1,0:T(8,128)(2,1)S(1)} %copy-done.15, bf16[512,2048]{1,0:T(8,128)(2,1)S(1)} %copy-done.16, bf16[512,1024]{1,0:T(8,128)(2,1)S(1)} %copy-done.32, bf16[512,1024]{1,0:T(8,128)(2,1)S(1)} %copy-done.20), kind=kOutput, calls=%fused_computation.29 | convolution fusion | flops 4309647360 | bytes 10485760 | tf_op jit(solution)/shard_map/dot_general | solution.py:51
  256.4 2.5 convert_reduce_fusion
  259.6 1.9 convolution_convert_fusion.6
  261.5 11.3 %collective-permute-done.5 = bf16[512,1024]{1,0:T(8,128)(2,1)} collective-permute-done((bf16[512,1024]{1,0:T(8,128)(2,1)S(1)}, bf16[512,1024]{1,0:T(8,128)(2,1)}, u32[]{:S(2)}, u32[]{:S(2)}) %collective-permute-start.5) | collective-permute-done | bytes 1048608 | tf_op jit(solution)/shard_map/ppermute | solution.py:510
  272.8 2.4 convolution_convert_fusion.5
  276.2 25.9 %shard_map.247 = (bf16[1024,512]{1,0:T(8,128)(2,1)S(1)}, bf16[1024,512]{1,0:T(8,128)(2,1)S(1)}, bf16[1024,512]{1,0:T(8,128)(2,1)S(1)}) custom-call(s32[1]{0:T(128)} %bitcast.flip_ref, f32[8]{0:T(128)S(1)} %multiply_exponential_fusion.slope_ref, bf16[1024,512]{1,0:T(8,128)(2,1)S(1)} %copy-done.3, bf16[1024,512]{1,0:T(8,128)(2,1)S(1)} %copy-done.5, ...), custom_call_target="tpu_custom_call" | custom-call | flops 10737418240 | bytes 7340032 | tf_op jit(solution)/shard_map/pallas_call | solution.py:159
  303.4 2.0 copy-done.26
  307.9 2.7 fusion.75
  310.6 3.7 convolution_convert_fusion
  314.3 2.6 pad_maximum_fusion
  316.9 13.5 %collective-permute-done.6 = bf16[512,1024]{1,0:T(8,128)(2,1)S(1)} collective-permute-done((bf16[512,1024]{1,0:T(8,128)(2,1)S(1)}, bf16[512,1024]{1,0:T(8,128)(2,1)S(1)}, u32[]{:S(2)}, u32[]{:S(2)}) %collective-permute-start.6) | collective-permute-done | bytes 1048608 | tf_op jit(solution)/shard_map/ppermute | solution.py:515
  330.4 3.7 fusion.38
  334.5 2.2 copy-done
  336.7 43.1 %shard_map.248 = (f32[64,2048]{1,0:T(8,128)S(1)}, f32[8,128]{1,0:T(8,128)S(1)}) custom-call(bf16[8,2,64,2048]{3,2,1,0:T(8,128)(2,1)S(1)} %bitcast.77, f32[2,2,8,8,128]{4,3,2,1,0:T(8,128)S(1)} %bitcast.78), custom_call_target="tpu_custom_call" | custom-call | bytes 8388608 | tf_op jit(solution)/shard_map/pallas_call | solution.py:449
  383.4 3.9 fusion.37
  (191 shorter events, 41.2 us)
Async XLA Ops:
  7.2 117.0 %all-gather.5.cloned.1.call-start = ((), (), s32[]{:S(2)}) async-start(), calls=%async_computation.3 | async-start | bytes 4456448 | tf_op jit(solution)/shard_map/all_gather | solution.py:503
  7.9 123.4 %all-gather.3.cloned.1.call-start = ((), (), s32[]{:S(2)}) async-start(), calls=%async_computation.2 | async-start | bytes 4456448 | tf_op jit(solution)/shard_map/all_gather | solution.py:503
  8.7 378.7 %reduce-scatter.5.cloned.1.call-start = ((), (), s32[]{:S(2)}) async-start(), calls=%async_computation.5 | async-start | bytes 4456448 | tf_op jit(solution)/shard_map/reduce_scatter | solution.py:506
  11.3 57.7 %copy-start.8 = (bf16[512,1024]{1,0:T(8,128)(2,1)S(1)}, bf16[512,1024]{1,0:T(8,128)(2,1)}, u32[]{:S(2)}) copy-start(bf16[512,1024]{1,0:T(8,128)(2,1)} %refs_2_.1) | copy-start | bytes 3145732
  77.2 14.8 %copy-start.1 = (bf16[1024,512]{1,0:T(8,128)(2,1)}, bf16[1024,512]{1,0:T(8,128)(2,1)S(1)}, u32[]{:S(2)}) copy-start(bf16[1024,512]{1,0:T(8,128)(2,1)S(1)} %get-tuple-element.86.v_ref) | copy-start | bytes 3145732
  77.2 14.8 %copy-start.2 = (bf16[1024,512]{1,0:T(8,128)(2,1)}, bf16[1024,512]{1,0:T(8,128)(2,1)S(1)}, u32[]{:S(2)}) copy-start(bf16[1024,512]{1,0:T(8,128)(2,1)S(1)} %get-tuple-element.87.q_ref) | copy-start | bytes 3145732
  77.2 14.8 %copy-start.4 = (bf16[1024,512]{1,0:T(8,128)(2,1)}, bf16[1024,512]{1,0:T(8,128)(2,1)S(1)}, u32[]{:S(2)}) copy-start(bf16[1024,512]{1,0:T(8,128)(2,1)S(1)} %get-tuple-element.88.k_ref) | copy-start | bytes 3145732
  92.0 30.7 %copy-start.6 = (bf16[1024,512]{1,0:T(8,128)(2,1)}, bf16[1024,512]{1,0:T(8,128)(2,1)S(1)}, u32[]{:S(2)}) copy-start(bf16[1024,512]{1,0:T(8,128)(2,1)S(1)} %shard_map.246) | copy-start | bytes 3145732
  93.8 26.3 %collective-permute-start = (bf16[512,1024]{1,0:T(8,128)(2,1)}, bf16[512,1024]{1,0:T(8,128)(2,1)}, u32[]{:S(2)}, u32[]{:S(2)}) collective-permute-start(bf16[512,1024]{1,0:T(8,128)(2,1)} %convolution_convert_fusion.2), channel_id=1, source_target_pairs={{0,1},{1,0},{2,3},{3,2},{4,5},{5,4},{6,7},{7,6},{8,9},{9,8},{10,11... | collective-permute-start | bytes 3145736 | tf_op jit(solution)/shard_map/ppermute | solution.py:515
  93.9 73.2 %collective-permute-start.3 = (bf16[512,1024]{1,0:T(8,128)(2,1)}, bf16[512,1024]{1,0:T(8,128)(2,1)}, u32[]{:S(2)}, u32[]{:S(2)}) collective-permute-start(bf16[512,1024]{1,0:T(8,128)(2,1)} %param.27), channel_id=1, source_target_pairs={{0,1},{1,0},{2,3},{3,2},{4,5},{5,4},{6,7},{7,6},{8,9},{9,8},{10,11... | collective-permute-start | bytes 3145736 | tf_op jit(solution)/shard_map/ppermute | solution.py:510
  124.1 7.2 %copy-start.19 = (bf16[512,1024]{1,0:T(8,128)(2,1)}, bf16[512,1024]{1,0:T(8,128)(2,1)S(1)}, u32[]{:S(2)}) copy-start(bf16[512,1024]{1,0:T(8,128)(2,1)S(1)} %add_convert_fusion.1) | copy-start | bytes 3145732
  124.1 40.6 %collective-permute-start.1 = (bf16[512,1024]{1,0:T(8,128)(2,1)S(1)}, bf16[512,1024]{1,0:T(8,128)(2,1)S(1)}, u32[]{:S(2)}, u32[]{:S(2)}) collective-permute-start(bf16[512,1024]{1,0:T(8,128)(2,1)S(1)} %add_convert_fusion.1), channel_id=1, source_target_pairs={{0,1},{1,0},{2,3},{3,2},{4,5},{5,4},{6,7},{7,6},{8,9},{9,8},{10,11... | collective-permute-start | bytes 3145736 | tf_op jit(solution)/shard_map/ppermute | solution.py:510
  131.3 33.4 %copy-start.30 = (bf16[1024,2048]{1,0:T(8,128)(2,1)S(1)}, bf16[1024,2048]{1,0:T(8,128)(2,1)}, u32[]{:S(2)}) copy-start(bf16[1024,2048]{1,0:T(8,128)(2,1)} %all-gather.3.cloned.1.call-done) | copy-start | bytes 12582916
  136.0 31.1 %copy-start.27 = (bf16[1024,2048]{1,0:T(8,128)(2,1)S(1)}, bf16[1024,2048]{1,0:T(8,128)(2,1)}, u32[]{:S(2)}) copy-start(bf16[1024,2048]{1,0:T(8,128)(2,1)} %all-gather.5.cloned.1.call-done) | copy-start | bytes 12582916
  136.0 31.1 %copy-start.33 = (f32[512,2048]{1,0:T(8,128)S(1)}, f32[512,2048]{1,0:T(8,128)}, u32[]{:S(2)}) copy-start(f32[512,2048]{1,0:T(8,128)} %fusion.101) | copy-start | bytes 12582916
  177.8 9.8 %copy-start.14 = (bf16[512,2048]{1,0:T(8,128)(2,1)}, bf16[512,2048]{1,0:T(8,128)(2,1)S(1)}, u32[]{:S(2)}) copy-start(bf16[512,2048]{1,0:T(8,128)(2,1)S(1)} %get-tuple-element.82) | copy-start | bytes 6291460
  187.5 201.6 %reduce-scatter.3.cloned.1.call-start = ((), (), s32[]{:S(2)}) async-start(), calls=%async_computation.4 | async-start | bytes 4456448 | tf_op jit(solution)/shard_map/reduce_scatter | solution.py:506
  187.6 6.1 %copy-start.28 = (bf16[1024,2048]{1,0:T(8,128)(2,1)S(1)}, bf16[1024,2048]{1,0:T(8,128)(2,1)}, u32[]{:S(2)}) copy-start(bf16[1024,2048]{1,0:T(8,128)(2,1)} %all-gather.5.cloned.1.call-done) | copy-start | bytes 12582916
  187.6 6.1 %copy-start.35 = (bf16[512,2048]{1,0:T(8,128)(2,1)S(1)}, bf16[512,2048]{1,0:T(8,128)(2,1)}, u32[]{:S(2)}) copy-start(bf16[512,2048]{1,0:T(8,128)(2,1)} %copy-done.34) | copy-start | bytes 6291460
  193.4 26.4 %copy-start.13 = (f32[512,1024]{1,0:T(8,128)S(1)}, f32[512,1024]{1,0:T(8,128)}, u32[]{:S(2)}) copy-start(f32[512,1024]{1,0:T(8,128)} %copy-done.12) | copy-start | bytes 6291460
  193.4 26.4 %collective-permute-start.4 = (bf16[512,1024]{1,0:T(8,128)(2,1)}, bf16[512,1024]{1,0:T(8,128)(2,1)}, u32[]{:S(2)}, u32[]{:S(2)}) collective-permute-start(bf16[512,1024]{1,0:T(8,128)(2,1)} %convolution_convert_fusion.3), channel_id=1, source_target_pairs={{0,1},{1,0},{2,3},{3,2},{4,5},{5,4},{6,7},{7,6},{8,9},{9,8},{10,11... | collective-permute-start | bytes 3145736 | tf_op jit(solution)/shard_map/ppermute | solution.py:515
  197.0 44.1 %collective-permute-start.2 = (bf16[512,1024]{1,0:T(8,128)(2,1)}, bf16[512,1024]{1,0:T(8,128)(2,1)}, u32[]{:S(2)}, u32[]{:S(2)}) collective-permute-start(bf16[512,1024]{1,0:T(8,128)(2,1)} %convolution_convert_fusion.4), channel_id=1, source_target_pairs={{0,1},{1,0},{2,3},{3,2},{4,5},{5,4},{6,7},{7,6},{8,9},{9,8},{10,11... | collective-permute-start | bytes 3145736 | tf_op jit(solution)/shard_map/ppermute | solution.py:515
  219.7 21.3 %copy-start.29 = (bf16[1024,2048]{1,0:T(8,128)(2,1)S(1)}, bf16[1024,2048]{1,0:T(8,128)(2,1)}, u32[]{:S(2)}) copy-start(bf16[1024,2048]{1,0:T(8,128)(2,1)} %all-gather.5.cloned.1.call-done) | copy-start | bytes 12582916
  219.7 21.3 %copy-start.37 = (bf16[512,2048]{1,0:T(8,128)(2,1)S(1)}, bf16[512,2048]{1,0:T(8,128)(2,1)}, u32[]{:S(2)}) copy-start(bf16[512,2048]{1,0:T(8,128)(2,1)} %copy-done.36) | copy-start | bytes 6291460
  241.1 8.0 %copy-start.16 = (bf16[512,2048]{1,0:T(8,128)(2,1)S(1)}, bf16[512,2048]{1,0:T(8,128)(2,1)}, u32[]{:S(2)}) copy-start(bf16[512,2048]{1,0:T(8,128)(2,1)} %get-tuple-element.107) | copy-start | bytes 6291460
  241.1 8.0 %copy-start.32 = (bf16[512,1024]{1,0:T(8,128)(2,1)S(1)}, bf16[512,1024]{1,0:T(8,128)(2,1)}, u32[]{:S(2)}) copy-start(bf16[512,1024]{1,0:T(8,128)(2,1)} %copy-done.31) | copy-start | bytes 3145732
  248.6 11.0 %copy-start.17 = (bf16[512,1024]{1,0:T(8,128)(2,1)}, bf16[512,1024]{1,0:T(8,128)(2,1)S(1)}, u32[]{:S(2)}) copy-start(bf16[512,1024]{1,0:T(8,128)(2,1)S(1)} %convert_element_type.129) | copy-start | bytes 3145732
  248.6 24.2 %collective-permute-start.5 = (bf16[512,1024]{1,0:T(8,128)(2,1)S(1)}, bf16[512,1024]{1,0:T(8,128)(2,1)}, u32[]{:S(2)}, u32[]{:S(2)}) collective-permute-start(bf16[512,1024]{1,0:T(8,128)(2,1)S(1)} %convert_element_type.129), channel_id=1, source_target_pairs={{0,1},{1,0},{2,3},{3,2},{4,5},{5,4},{6,7},{7,6},{8,9},{9,8},{10,11... | collective-permute-start | bytes 3145736 | tf_op jit(solution)/shard_map/ppermute | solution.py:510
  261.5 14.7 %copy-start.3 = (bf16[1024,512]{1,0:T(8,128)(2,1)S(1)}, bf16[1024,512]{1,0:T(8,128)(2,1)}, u32[]{:S(2)}) copy-start(bf16[1024,512]{1,0:T(8,128)(2,1)} %copy-done.2) | copy-start | bytes 3145732
  261.5 14.7 %copy-start.5 = (bf16[1024,512]{1,0:T(8,128)(2,1)S(1)}, bf16[1024,512]{1,0:T(8,128)(2,1)}, u32[]{:S(2)}) copy-start(bf16[1024,512]{1,0:T(8,128)(2,1)} %copy-done.4) | copy-start | bytes 3145732
  307.3 23.2 %collective-permute-start.6 = (bf16[512,1024]{1,0:T(8,128)(2,1)S(1)}, bf16[512,1024]{1,0:T(8,128)(2,1)S(1)}, u32[]{:S(2)}, u32[]{:S(2)}) collective-permute-start(bf16[512,1024]{1,0:T(8,128)(2,1)S(1)} %fusion.70), channel_id=1, source_target_pairs={{0,1},{1,0},{2,3},{3,2},{4,5},{5,4},{6,7},{7,6},{8,9},{9,8},{10,11... | collective-permute-start | bytes 3145736 | tf_op jit(solution)/shard_map/ppermute | solution.py:515
  314.3 16.1 %copy-start.9 = (bf16[512,1024]{1,0:T(8,128)(2,1)S(1)}, bf16[512,1024]{1,0:T(8,128)(2,1)}, u32[]{:S(2)}) copy-start(bf16[512,1024]{1,0:T(8,128)(2,1)} %refs_2_.1) | copy-start | bytes 3145732
  (17 other events, 41.8 us)
Sparse Core Ops, SparseCore 0:
  10.2 58.1 all-gather.4
  70.5 52.1 all-gather.2
  187.6 75.6 reduce-scatter.4
  267.5 71.3 reduce-scatter.2

commit v3 on v2

--- a/solution.py
+++ b/solution.py
@@ -211,8 +211,8 @@
 def gather_kernel(chips, parts, *refs):
     pair = parts == 2
     if pair:
-        x_ref, small_ref, tok_ref, full_ref, all_ref, other_ref = refs[:6]
-        sems = refs[6:]
+        x_ref, small_ref, tok_ref, cot_ref, full_ref, all_ref, other_ref, other_cot_ref = refs[:8]
+        sems = refs[8:]
     else:
         x_ref, small_ref, full_ref, all_ref = refs[:4]
         sems = refs[4:]
@@ -267,6 +267,9 @@
             copy = remote(src, dst, big_s.at[slot], big_r.at[slot], device)
             copy.start()
             started.append(copy)
+        if pair and step == 1:
+            cot = remote(cot_ref, other_cot_ref, tok_s.at[1], tok_r.at[1], peers[0])
+            cot.start()
         if step == 0:
             swap(mine, True)
         else:
@@ -294,9 +297,10 @@
         copy.wait()
     if pair:
         tok.wait()
-
-
-def gather_call(shard, small, tokens, chips, parts):
+        cot.wait()
+
+
+def gather_call(shard, small, tokens, cotangent, chips, parts):
     rows, columns = shard.shape
     anywhere = pl.BlockSpec(memory_space=pl.ANY)
     out = [
@@ -305,8 +309,8 @@
     ]
     operands = [shard, small]
     if parts == 2:
-        out.append(jax.ShapeDtypeStruct(tokens.shape, BF16))
-        operands.append(tokens)
+        out += [jax.ShapeDtypeStruct(tokens.shape, BF16)] * 2
+        operands += [tokens, cotangent]
     sem = pltpu.SemaphoreType.DMA
     result = pl.pallas_call(
         functools.partial(gather_kernel, chips, parts),
@@ -316,13 +320,13 @@
         scratch_shapes=[sem((2,))]
         + [sem((chips,))] * 8
         + [sem((parts - 1,))] * 2
-        + [sem((1,))] * 2,
+        + [sem((2,))] * 2,
         compiler_params=pltpu.CompilerParams(collective_id=0, has_side_effects=True),
         cost_estimate=pl.CostEstimate(
             flops=0, bytes_accessed=64 * rows * columns, transcendentals=0
         ),
     )(*operands)
-    return list(result) + [None] * (3 - len(out))
+    return list(result) + [None] * (4 - len(out))
 
 
 def reduce_kernel(chips, parts, g_ref, s_ref, o_ref, so_ref, *scratch):
@@ -359,16 +363,30 @@
         chip = ring_chip(place + shift, chips)
         return g_ref[chip, core].astype(F32) + pair_in[n].astype(F32)
 
-    for copy in ten:
-        copy.wait_recv()
-    total = s_ref[tensor]
-    for k in range(len(peers)):
-        total = total + sm_ten[k]
-    sm_sum[...] = total
-    sm_pair_copy = remote(sm_sum.at[away], sm_pair, smp_s.at[0], smp_r.at[0], twin)
-    sm_pair_copy.start()
     sends = list(ten)
     arrived = {}
+    small_arrived = {}
+
+    def own_small(shift):
+        chip = ring_chip(place + shift, chips)
+        return sm_sum[core, chip] + sm_pair[chip]
+
+    def small_step(step):
+        for side, device in ((0, left), (1, right)):
+            if step == 0 and side == 1:
+                continue
+            shift = (step - steps) if side == 0 else (steps - step)
+            slot = side * steps + step
+            value = own_small(shift)
+            if side in small_arrived:
+                small_arrived[side].wait_recv()
+                value = value + sm_in[slot - 1]
+            sm_out[slot] = value
+            copy = remote(sm_out.at[slot], sm_in.at[slot], sm_s.at[slot], sm_r.at[slot], device)
+            copy.start()
+            small_arrived[side] = copy
+            sends.append(copy)
+
     for step in range(steps):
         for side, device in ((0, left), (1, right)):
             shift = (step - steps) if side == 0 else (steps - step)
@@ -401,29 +419,21 @@
             copy.start()
             arrived[side] = copy
             sends.append(copy)
-    sm_pair_copy.wait_recv()
-    kept = {}
-    small_arrived = {}
-
-    def own_small(shift):
-        chip = ring_chip(place + shift, chips)
-        return sm_sum[core, chip] + sm_pair[chip]
-
-    for step in range(steps):
-        for side, device in ((0, left), (1, right)):
-            if step == 0 and side == 1:
-                continue
-            shift = (step - steps) if side == 0 else (steps - step)
-            slot = side * steps + step
-            value = own_small(shift)
-            if side in small_arrived:
-                small_arrived[side].wait_recv()
-                value = value + sm_in[slot - 1]
-            sm_out[slot] = value
-            copy = remote(sm_out.at[slot], sm_in.at[slot], sm_s.at[slot], sm_r.at[slot], device)
-            copy.start()
-            small_arrived[side] = copy
-            sends.append(copy)
+        if step == 0:
+            for copy in ten:
+                copy.wait_recv()
+            total = s_ref[tensor]
+            for k in range(len(peers)):
+                total = total + sm_ten[k]
+            sm_sum[...] = total
+            sm_pair_copy = remote(sm_sum.at[away], sm_pair, smp_s.at[0], smp_r.at[0], twin)
+            sm_pair_copy.start()
+        elif step == 1:
+            sm_pair_copy.wait_recv()
+            small_step(0)
+        else:
+            small_step(step - 1)
+    small_step(steps - 1)
     value = own(0)
     for side in range(2):
         arrived[side].wait_recv()
@@ -536,8 +546,8 @@
     tile = (8, 128)
     pad = tile[0] * tile[1] - packed.size
     first_shard = jnp.concatenate([w_qkv[0], w_qkv[1], w_qkv[2], w_out.T], axis=1)
-    first_full, small, other_tokens = gather_call(
-        first_shard, jnp.pad(packed, (0, pad)).reshape(tile), tokens, chips, parts
+    first_full, small, other_tokens, other_cot = gather_call(
+        first_shard, jnp.pad(packed, (0, pad)).reshape(tile), tokens, cotangent, chips, parts
     )
     first_full = first_full.reshape(-1, first_shard.shape[1])
     small = small.reshape(parts, n_dp, -1).transpose(1, 0, 2).reshape(everyone, -1)
@@ -578,7 +588,7 @@
     slopes = jnp.exp2(-8.0 * (head_ids + 1).astype(F32) / H)
     flip = (t_index if parts == 2 else 0 * t_index).astype(jnp.int32).reshape(1)
 
-    cot_blocks = gather_rows(cotangent)
+    cot_blocks = [cotangent, other_cot] if parts == 2 else gather_rows(cotangent)
     inputs = tokens.astype(F32)
     normed_one, inverse_one = normalize(inputs)
     low_one = (normed_one * gain_a + shift_a).astype(BF16)
@@ -616,7 +626,6 @@
         jax.vjp(smooth_gate, h)[1](g)[0].astype(BF16) for h, g in zip(hidden, grad_gated)
     ]
     grad_two = scatter_rows(lambda b: mm_t(b, up_full), grad_hidden)
-    output = middle + scatter_rows(lambda b: mm_t(b, down_t), gated) + down_shift
 
     cot_all = joined(cot_blocks)
     grad_hidden_all = joined(grad_hidden)
@@ -632,6 +641,15 @@
     grad_out_shift = jnp.sum(grad_middle, axis=0)
     low_blocks = gather_rows(grad_middle.astype(BF16))
     grad_attended = joined([mm(b, out_t).astype(BF16) for b in low_blocks])
+    if parts == 2:
+        late = lax.optimization_barrier((*gated, low_blocks[1]))[:2]
+        away = mm_t(late[1], down_t).astype(BF16)
+        grad_attended, away = lax.optimization_barrier((grad_attended, away))
+        came = lax.ppermute(away, "tensor", [(0, 1), (1, 0)])
+        feed = mm_t(late[0], down_t) + came.astype(F32)
+    else:
+        feed = scatter_rows(lambda b: mm_t(b, down_t), gated)
+    output = middle + feed + down_shift
     scratch = [vmem, vmem] + [pltpu.VMEM((length, PAIR), F32)] * 2
     grad_qkv_parts = attention_call(
         attend_back_kernel,

time: 403 us -> 386 us (0.958)
  waiting for transfers between devices: 114 us -> 101 us
  Pallas kernels: 136 us -> 130 us
    ppermute x3 -> x2, waiting for transfers between devices: 40 us -> 21.6 us  [gather_rows(): return [mine, lax.ppermute(mine, 'tensor', [(0, 1), (1, 0)])]]
    pallas_call x1, Pallas kernels: 43.1 us -> 37.9 us  [reduce_call(): pl.pallas_call(functools.partial(reduce_kernel, chips, parts), out_shape=...]
    ppermute x4 -> x3, waiting for transfers between devices: 73 us -> 77.7 us  [scatter_rows(): lax.ppermute(product(blocks[1]).astype(BF16), 'tensor', [(0, 1), (1, 0)])]
    unnamed x82 -> x76, local copies, waits for them, and re-layouts: 12.9 us -> 12.7 us
  transfers between devices with their start and end apart: 11 -> 10, of which waited for: 6 -> 5; matrix products, arithmetic and copies ran while one was open for 24% -> 26% of each run, Pallas kernels for 34% -> 34%
where the time goes in v3:
time: 386 us; the launch traced here: 380 us
  Pallas kernels  130 us (34%)
  waiting for transfers between devices  101 us (26%)
  matrix products  85.3 us (22%)
  other arithmetic  23.4 us (6%)
  local copies, waits for them, and re-layouts  22.3 us (6%)
  between operations  14.7 us (4%)
    ppermute x3, waiting for transfers between devices, scatter_rows(): lax.ppermute(product(blocks[1]).astype(BF16), 'tensor', [(0, 1), (1, 0)])  77.7 us
    pallas_call x1, Pallas kernels, gather_call(): pl.pallas_call(functools.partial(gather_kernel, chips, parts), out_shape=...  51.8 us
    pallas_call x2, Pallas kernels, attention_call(): pl.pallas_call(kernel, grid=(group // length, width // PAIR), out_shape=[...  40.4 us
    pallas_call x1, Pallas kernels, reduce_call(): pl.pallas_call(functools.partial(reduce_kernel, chips, parts), out_shape=...  37.9 us
    dot_general x8, matrix products, mm(): lax.dot_general(a, b, (((1,), (0,)), ((), ())), preferred_element_type=F32)  33.1 us
    dot_general x8, matrix products, mm_t(): lax.dot_general(a, b, (((1,), (1,)), ((), ())), preferred_element_type=F32)  31.6 us
    ppermute x2, waiting for transfers between devices, gather_rows(): return [mine, lax.ppermute(mine, 'tensor', [(0, 1), (1, 0)])]  21.6 us
    dot_general x4, matrix products, t_mm(): lax.dot_general(a, b, (((0,), (0,)), ((), ())), preferred_element_type=F32)  20.6 us
  transfers between devices with their start and end apart: 10, of which 5 were waited for; matrix products, arithmetic and copies ran while one was open for 26% of the time, Pallas kernels for 34%

profile of v3, /device:TPU:0, one launch (start us, length us, event | category | flops | bytes accessed | tf_op | source)
XLA Modules:
  0.0 380.3 jit_solution(12983346045741350229)
XLA Ops:
  14.3 51.8 %shard_map.245 = (bf16[8,2,64,2048]{3,2,1,0:T(8,128)(2,1)}, f32[2,8,2,8,128]{4,3,2,1,0:T(8,128)}, bf16[512,1024]{1,0:T(8,128)(2,1)}, bf16[512,1024]{1,0:T(8,128)(2,1)}) custom-call(bf16[64,2048]{1,0:T(8,128)(2,1)} %pad_maximum_fusion.6.refs_0_, f32[8,128]{1,0:T(8,128)} %pad_bitcast_fusion.1.refs_1_, bf16[512,1024]{1,0:T(8,128)(2,1)} %refs_2_.1, ...), custom_call_target="tpu_custom_call" | custom-call | bytes 8388608 | tf_op jit(solution)/shard_map/pallas_call | solution.py:315
  70.6 2.1 copy-done.26
  76.6 14.5 %shard_map.246 = bf16[1024,512]{1,0:T(8,128)(2,1)S(1)} custom-call(s32[1]{0:T(128)} %bitcast.flip_ref, f32[8]{0:T(128)S(1)} %multiply_exponential_fusion.slope_ref, bf16[1024,512]{1,0:T(8,128)(2,1)S(1)} %get-tuple-element.97.q_ref, bf16[1024,512]{1,0:T(8,128)(2,1)S(1)} %get-tuple-element.98.k_ref, bf16[1024,512]{1,0:T(8,128)(2,1)S(1)} %get-tuple-element.96.v_ref), custom_call_target="tpu_custom_call" | custom-call | flops 4294967296 | bytes 4194304 | tf_op jit(solution)/shard_map/pallas_call | solution.py:159
  94.3 24.9 %collective-permute-done = bf16[512,1024]{1,0:T(8,128)(2,1)} collective-permute-done((bf16[512,1024]{1,0:T(8,128)(2,1)}, bf16[512,1024]{1,0:T(8,128)(2,1)}, u32[]{:S(2)}, u32[]{:S(2)}) %collective-permute-start) | collective-permute-done | bytes 1048608 | tf_op jit(solution)/shard_map/ppermute | solution.py:525
  119.2 2.6 fusion.98
  123.8 6.5 %fusion.100 = f32[512,2048]{1,0:T(8,128)} fusion(bf16[512,1024]{1,0:T(8,128)(2,1)S(1)} %copy-done.15, bf16[1024,2048]{1,0:T(8,128)(2,1)} %all-gather.5.cloned.1.call-done), kind=kOutput, calls=%fused_computation.165 | convolution fusion | flops 2147483648 | bytes 9437184 | tf_op jit(solution)/shard_map/dot_general | solution.py:43
  130.3 4.7 %fusion.99 = f32[512,2048]{1,0:T(8,128)S(1)} fusion(bf16[512,1024]{1,0:T(8,128)(2,1)S(1)} %add_convert_fusion.1, bf16[1024,2048]{1,0:T(8,128)(2,1)} %all-gather.3.cloned.1.call-done), kind=kOutput, calls=%fused_computation.164 | convolution fusion | flops 2147483648 | bytes 9437184 | tf_op jit(solution)/shard_map/dot_general | solution.py:43
  135.0 2.4 fusion.101
  137.4 10.9 %collective-permute-done.1 = bf16[512,1024]{1,0:T(8,128)(2,1)} collective-permute-done((bf16[512,1024]{1,0:T(8,128)(2,1)S(1)}, bf16[512,1024]{1,0:T(8,128)(2,1)}, u32[]{:S(2)}, u32[]{:S(2)}) %collective-permute-start.1) | collective-permute-done | bytes 1048608 | tf_op jit(solution)/shard_map/ppermute | solution.py:520
  148.3 11.3 %multiply_convert_fusion = (bf16[512,2048]{1,0:T(8,128)(2,1)}, bf16[512,2048]{1,0:T(8,128)(2,1)S(1)}, bf16[512,2048]{1,0:T(8,128)(2,1)S(1)}, bf16[512,2048]{1,0:T(8,128)(2,1)}) fusion(f32[2048]{0:T(1024)S(1)} %add.185, f32[512,2048]{1,0:T(8,128)S(1)} %fusion.101, f32[512,2048]{1,0:T(8,128)S(1)} %copy-done.31, f32[512,2048]{1,0:T(8,128)S(1)} %fusion.99, ...), kind=kOutput, calls=%fused_computation.25 | convolution fusion | flops 2195718144 | bytes 26222592 | tf_op jit(solution)/shard_map/dot_general | solution.py:43
  161.5 7.4 %convolution_convert_fusion.1 = bf16[1024,2048]{1,0:T(8,128)(2,1)} fusion(bf16[512,2048]{1,0:T(8,128)(2,1)S(1)} %get-tuple-element.93, bf16[512,2048]{1,0:T(8,128)(2,1)S(1)} %get-tuple-element.115, bf16[512,1024]{1,0:T(8,128)(2,1)} %collective-permute-done.1, bf16[512,1024]{1,0:T(8,128)(2,1)S(1)} %add_convert_fusion.1), kind=kOutput, calls=%fused_computation.29 | convolution fusion | flops 4309647360 | bytes 10485760 | tf_op jit(solution)/shard_map/dot_general | solution.py:51
  169.0 6.3 %convolution_convert_fusion.4 = bf16[512,1024]{1,0:T(8,128)(2,1)} fusion(bf16[512,2048]{1,0:T(8,128)(2,1)} %copy-done.16, bf16[1024,2048]{1,0:T(8,128)(2,1)} %all-gather.3.cloned.1.call-done), kind=kOutput, calls=%fused_computation.104 | convolution fusion | flops 2148007936 | bytes 7340032 | tf_op jit(solution)/shard_map/dot_general | solution.py:47
  175.8 24.1 %collective-permute-done.2 = bf16[512,1024]{1,0:T(8,128)(2,1)} collective-permute-done((bf16[512,1024]{1,0:T(8,128)(2,1)}, bf16[512,1024]{1,0:T(8,128)(2,1)}, u32[]{:S(2)}, u32[]{:S(2)}) %collective-permute-start.2) | collective-permute-done | bytes 1048608 | tf_op jit(solution)/shard_map/ppermute | solution.py:525
  199.9 6.7 %multiply_reduce_fusion = (f32[1024]{0:T(1024)S(1)}, f32[512]{0:T(512)S(1)}, f32[512]{0:T(512)S(1)}, f32[1024]{0:T(1024)S(1)}, f32[512,1024]{1,0:T(8,128)S(1)}) fusion(f32[512,1024]{1,0:T(8,128)S(1)} %copy-done.11, f32[512]{0:T(512)S(1)} %add_rsqrt_fusion, f32[512]{0:T(512)S(1)} %broadcast_multiply_fusion.4, bf16[512,1024]{1,0:T(8,128)(2,1)} %collective-permute-done.2, ...), kind=kOutput, calls=%fused_computation.82 | convolution fusion | flops 2153247744 | bytes 11554816 | tf_op jit(solution)/shard_map/dot_general | solution.py:47
  206.6 2.5 fusion.94
  212.1 6.2 %fusion.18 = bf16[1024,2048]{1,0:T(8,128)(2,1)} fusion(bf16[512,2048]{1,0:T(8,128)(2,1)S(1)} %copy-done.33, bf16[512,2048]{1,0:T(8,128)(2,1)S(1)} %copy-done.32, bf16[512,1024]{1,0:T(8,128)(2,1)S(1)} %copy-done.30, bf16[512,1024]{1,0:T(8,128)(2,1)S(1)} %copy-done.15), kind=kOutput, calls=%fused_computation.27 | convolution fusion | flops 4309647360 | bytes 10485760 | tf_op jit(solution)/shard_map/dot_general | solution.py:51
  218.4 2.5 convert_reduce_fusion
  221.5 2.4 convolution_convert_fusion.6
  224.0 10.6 %collective-permute-done.3 = bf16[512,1024]{1,0:T(8,128)(2,1)} collective-permute-done((bf16[512,1024]{1,0:T(8,128)(2,1)}, bf16[512,1024]{1,0:T(8,128)(2,1)}, u32[]{:S(2)}, u32[]{:S(2)}) %collective-permute-start.3) | collective-permute-done | bytes 1048608 | tf_op jit(solution)/shard_map/ppermute | solution.py:520
  234.6 2.3 convolution_convert_fusion.5
  237.9 3.4 convolution_convert_fusion.3
  241.3 25.8 %shard_map.247 = (bf16[1024,512]{1,0:T(8,128)(2,1)S(1)}, bf16[1024,512]{1,0:T(8,128)(2,1)S(1)}, bf16[1024,512]{1,0:T(8,128)(2,1)S(1)}) custom-call(s32[1]{0:T(128)} %bitcast.flip_ref, f32[8]{0:T(128)S(1)} %multiply_exponential_fusion.slope_ref, bf16[1024,512]{1,0:T(8,128)(2,1)S(1)} %copy-done.3, bf16[1024,512]{1,0:T(8,128)(2,1)S(1)} %copy-done.5, ...), custom_call_target="tpu_custom_call" | custom-call | flops 10737418240 | bytes 7340032 | tf_op jit(solution)/shard_map/pallas_call | solution.py:159
  268.7 2.1 copy-done.27
  274.5 3.0 fusion.75
  277.5 3.9 %convolution_convert_fusion = bf16[1024,1536]{1,0:T(8,128)(2,1)S(1)} fusion(bf16[1024,1536]{1,0:T(8,128)(2,1)S(1)} %constant_dynamic-update-slice_fusion, bf16[512,1024]{1,0:T(8,128)(2,1)S(1)} %copy-done.20, bf16[512,1024]{1,0:T(8,128)(2,1)S(1)} %copy-done.22), kind=kOutput, calls=%fused_computation.28 | convolution fusion | flops 3226992640 | bytes 8388608 | tf_op jit(solution)/shard_map/dot_general | solution.py:51
  281.4 2.6 pad_maximum_fusion
  284.0 28.6 %collective-permute-done.5 = bf16[512,1024]{1,0:T(8,128)(2,1)S(1)} collective-permute-done((bf16[512,1024]{1,0:T(8,128)(2,1)S(1)}, bf16[512,1024]{1,0:T(8,128)(2,1)S(1)}, u32[]{:S(2)}, u32[]{:S(2)}) %collective-permute-start.5) | collective-permute-done | bytes 1048608 | tf_op jit(solution)/shard_map/ppermute | solution.py:525
  312.7 3.7 fusion.38
  316.7 2.2 copy-done
  318.9 37.9 %shard_map.248 = (f32[64,2048]{1,0:T(8,128)S(1)}, f32[8,128]{1,0:T(8,128)S(1)}) custom-call(bf16[8,2,64,2048]{3,2,1,0:T(8,128)(2,1)S(1)} %bitcast.77, f32[2,2,8,8,128]{4,3,2,1,0:T(8,128)S(1)} %bitcast.78), custom_call_target="tpu_custom_call" | custom-call | bytes 8388608 | tf_op jit(solution)/shard_map/pallas_call | solution.py:459
  360.5 4.1 %fusion.37 = bf16[512,1024]{1,0:T(8,128)(2,1)} fusion(f32[512,1024]{1,0:T(8,128)} %copy-done.13, bf16[512,1024]{1,0:T(8,128)(2,1)S(1)} %copy-done.9, f32[512,1024]{1,0:T(8,128)} %get-tuple-element.128, f32[512]{0:T(512)S(1)} %broadcast_multiply_fusion, f32[512]{0:T(512)S(1)} %broadcast_multiply_fusion.1, f32[1024]{0:T(1024)S(1)} %mul.205, ...), kind=kLoop, calls=%fused_computation.59 | loop fusion | flops 5242880 | bytes 6303744 | tf_op jit(solution)/shard_map/convert_element_type | solution.py:725
  364.6 5.4 %add_convert_fusion = bf16[512,1024]{1,0:T(8,128)(2,1)} fusion(f32[512,1024]{1,0:T(8,128)S(1)} %copy-done.12, bf16[512,1024]{1,0:T(8,128)(2,1)} %collective-permute-done.4, bf16[512,2048]{1,0:T(8,128)(2,1)} %get-tuple-element.31, bf16[1024,2048]{1,0:T(8,128)(2,1)S(1)} %copy-done.25, f32[1024]{0:T(1024)S(1)} %add.197), kind=kOutput, calls=%fused_computation.84 | convolution fusion | flops 2150105088 | bytes 10489856 | tf_op jit(solution)/shard_map/dot_general | solution.py:47
  (184 shorter events, 40.2 us)
Async XLA Ops:
  7.2 116.2 %all-gather.5.cloned.1.call-start = ((), (), s32[]{:S(2)}) async-start(), calls=%async_computation.3 | async-start | bytes 4456448 | tf_op jit(solution)/shard_map/all_gather | solution.py:513
  7.9 122.3 %all-gather.3.cloned.1.call-start = ((), (), s32[]{:S(2)}) async-start(), calls=%async_computation.2 | async-start | bytes 4456448 | tf_op jit(solution)/shard_map/all_gather | solution.py:513
  8.7 361.4 %reduce-scatter.3.cloned.1.call-start = ((), (), s32[]{:S(2)}) async-start(), calls=%async_computation.4 | async-start | bytes 4456448 | tf_op jit(solution)/shard_map/reduce_scatter | solution.py:516
  14.3 54.1 %copy-start.8 = (bf16[512,1024]{1,0:T(8,128)(2,1)S(1)}, bf16[512,1024]{1,0:T(8,128)(2,1)}, u32[]{:S(2)}) copy-start(bf16[512,1024]{1,0:T(8,128)(2,1)} %refs_2_.1) | copy-start | bytes 3145732
  70.5 3.9 %copy-start.19 = (bf16[512,1024]{1,0:T(8,128)(2,1)}, bf16[512,1024]{1,0:T(8,128)(2,1)S(1)}, u32[]{:S(2)}) copy-start(bf16[512,1024]{1,0:T(8,128)(2,1)S(1)} %get-tuple-element.117) | copy-start | bytes 3145732
  70.5 3.9 %copy-start.21 = (bf16[512,1024]{1,0:T(8,128)(2,1)}, bf16[512,1024]{1,0:T(8,128)(2,1)S(1)}, u32[]{:S(2)}) copy-start(bf16[512,1024]{1,0:T(8,128)(2,1)S(1)} %get-tuple-element.118) | copy-start | bytes 3145732
  76.5 14.6 %copy-start.1 = (bf16[1024,512]{1,0:T(8,128)(2,1)}, bf16[1024,512]{1,0:T(8,128)(2,1)S(1)}, u32[]{:S(2)}) copy-start(bf16[1024,512]{1,0:T(8,128)(2,1)S(1)} %get-tuple-element.96.v_ref) | copy-start | bytes 3145732
  76.6 14.6 %copy-start.2 = (bf16[1024,512]{1,0:T(8,128)(2,1)}, bf16[1024,512]{1,0:T(8,128)(2,1)S(1)}, u32[]{:S(2)}) copy-start(bf16[1024,512]{1,0:T(8,128)(2,1)S(1)} %get-tuple-element.97.q_ref) | copy-start | bytes 3145732
  76.6 14.6 %copy-start.4 = (bf16[1024,512]{1,0:T(8,128)(2,1)}, bf16[1024,512]{1,0:T(8,128)(2,1)S(1)}, u32[]{:S(2)}) copy-start(bf16[1024,512]{1,0:T(8,128)(2,1)S(1)} %get-tuple-element.98.k_ref) | copy-start | bytes 3145732
  91.2 30.6 %copy-start.6 = (bf16[1024,512]{1,0:T(8,128)(2,1)}, bf16[1024,512]{1,0:T(8,128)(2,1)S(1)}, u32[]{:S(2)}) copy-start(bf16[1024,512]{1,0:T(8,128)(2,1)S(1)} %shard_map.246) | copy-start | bytes 3145732
  92.9 26.3 %collective-permute-start = (bf16[512,1024]{1,0:T(8,128)(2,1)}, bf16[512,1024]{1,0:T(8,128)(2,1)}, u32[]{:S(2)}, u32[]{:S(2)}) collective-permute-start(bf16[512,1024]{1,0:T(8,128)(2,1)} %convolution_convert_fusion.2), channel_id=1, source_target_pairs={{0,1},{1,0},{2,3},{3,2},{4,5},{5,4},{6,7},{7,6},{8,9},{9,8},{10,11... | collective-permute-start | bytes 3145736 | tf_op jit(solution)/shard_map/ppermute | solution.py:525
  123.1 25.2 %collective-permute-start.1 = (bf16[512,1024]{1,0:T(8,128)(2,1)S(1)}, bf16[512,1024]{1,0:T(8,128)(2,1)}, u32[]{:S(2)}, u32[]{:S(2)}) collective-permute-start(bf16[512,1024]{1,0:T(8,128)(2,1)S(1)} %add_convert_fusion.1), channel_id=1, source_target_pairs={{0,1},{1,0},{2,3},{3,2},{4,5},{5,4},{6,7},{7,6},{8,9},{9,8},{10,11... | collective-permute-start | bytes 3145736 | tf_op jit(solution)/shard_map/ppermute | solution.py:520
  130.3 4.7 %copy-start.29 = (bf16[512,1024]{1,0:T(8,128)(2,1)S(1)}, bf16[512,1024]{1,0:T(8,128)(2,1)}, u32[]{:S(2)}) copy-start(bf16[512,1024]{1,0:T(8,128)(2,1)} %get-tuple-element.30) | copy-start | bytes 3145732
  130.3 4.7 %copy-start.23 = (bf16[1024,2048]{1,0:T(8,128)(2,1)S(1)}, bf16[1024,2048]{1,0:T(8,128)(2,1)}, u32[]{:S(2)}) copy-start(bf16[1024,2048]{1,0:T(8,128)(2,1)} %all-gather.5.cloned.1.call-done) | copy-start | bytes 12582916
  135.0 13.3 %copy-start.28 = (bf16[1024,2048]{1,0:T(8,128)(2,1)S(1)}, bf16[1024,2048]{1,0:T(8,128)(2,1)}, u32[]{:S(2)}) copy-start(bf16[1024,2048]{1,0:T(8,128)(2,1)} %all-gather.3.cloned.1.call-done) | copy-start | bytes 12582916
  135.0 13.3 %copy-start.31 = (f32[512,2048]{1,0:T(8,128)S(1)}, f32[512,2048]{1,0:T(8,128)}, u32[]{:S(2)}) copy-start(f32[512,2048]{1,0:T(8,128)} %fusion.100) | copy-start | bytes 12582916
  169.0 30.9 %copy-start.11 = (f32[512,1024]{1,0:T(8,128)S(1)}, f32[512,1024]{1,0:T(8,128)}, u32[]{:S(2)}) copy-start(f32[512,1024]{1,0:T(8,128)} %copy-done.10) | copy-start | bytes 6291460
  169.0 202.8 %reduce-scatter.5.cloned.1.call-start = ((), (), s32[]{:S(2)}) async-start(), calls=%async_computation.5 | async-start | bytes 4456448 | tf_op jit(solution)/shard_map/reduce_scatter | solution.py:516
  175.3 24.6 %collective-permute-start.2 = (bf16[512,1024]{1,0:T(8,128)(2,1)}, bf16[512,1024]{1,0:T(8,128)(2,1)}, u32[]{:S(2)}, u32[]{:S(2)}) collective-permute-start(bf16[512,1024]{1,0:T(8,128)(2,1)} %convolution_convert_fusion.4), channel_id=1, source_target_pairs={{0,1},{1,0},{2,3},{3,2},{4,5},{5,4},{6,7},{7,6},{8,9},{9,8},{10,11... | collective-permute-start | bytes 3145736 | tf_op jit(solution)/shard_map/ppermute | solution.py:525
  206.6 5.0 %copy-start.33 = (bf16[512,2048]{1,0:T(8,128)(2,1)S(1)}, bf16[512,2048]{1,0:T(8,128)(2,1)}, u32[]{:S(2)}) copy-start(bf16[512,2048]{1,0:T(8,128)(2,1)} %get-tuple-element.32) | copy-start | bytes 6291460
  211.5 23.1 %collective-permute-start.3 = (bf16[512,1024]{1,0:T(8,128)(2,1)}, bf16[512,1024]{1,0:T(8,128)(2,1)}, u32[]{:S(2)}, u32[]{:S(2)}) collective-permute-start(bf16[512,1024]{1,0:T(8,128)(2,1)} %convert_element_type.126), channel_id=1, source_target_pairs={{0,1},{1,0},{2,3},{3,2},{4,5},{5,4},{6,7},{7,6},{8,9},{9,8},{10,11... | collective-permute-start | bytes 3145736 | tf_op jit(solution)/shard_map/ppermute | solution.py:520
  212.1 6.2 %copy-start.17 = (bf16[512,2048]{1,0:T(8,128)(2,1)S(1)}, bf16[512,2048]{1,0:T(8,128)(2,1)}, u32[]{:S(2)}) copy-start(bf16[512,2048]{1,0:T(8,128)(2,1)} %copy-done.16) | copy-start | bytes 6291460
  221.5 16.4 %copy-start.34 = (bf16[512,2048]{1,0:T(8,128)(2,1)S(1)}, bf16[512,2048]{1,0:T(8,128)(2,1)}, u32[]{:S(2)}) copy-start(bf16[512,2048]{1,0:T(8,128)(2,1)} %get-tuple-element.32) | copy-start | bytes 6291460
  224.0 14.0 %copy-start.24 = (bf16[1024,2048]{1,0:T(8,128)(2,1)S(1)}, bf16[1024,2048]{1,0:T(8,128)(2,1)}, u32[]{:S(2)}) copy-start(bf16[1024,2048]{1,0:T(8,128)(2,1)} %all-gather.5.cloned.1.call-done) | copy-start | bytes 12582916
  237.9 3.4 copy-start.3
  237.9 3.4 copy-start.5
  268.1 96.5 %collective-permute-start.4 = (bf16[512,1024]{1,0:T(8,128)(2,1)}, bf16[512,1024]{1,0:T(8,128)(2,1)}, u32[]{:S(2)}, u32[]{:S(2)}) collective-permute-start(bf16[512,1024]{1,0:T(8,128)(2,1)} %convolution_convert_fusion.3), channel_id=1, source_target_pairs={{0,1},{1,0},{2,3},{3,2},{4,5},{5,4},{6,7},{7,6},{8,9},{9,8},{10,11... | collective-permute-start | bytes 3145736 | tf_op jit(solution)/shard_map/ppermute | solution.py:648
  270.7 3.7 copy-start.7
  272.6 40.1 %collective-permute-start.5 = (bf16[512,1024]{1,0:T(8,128)(2,1)S(1)}, bf16[512,1024]{1,0:T(8,128)(2,1)S(1)}, u32[]{:S(2)}, u32[]{:S(2)}) collective-permute-start(bf16[512,1024]{1,0:T(8,128)(2,1)S(1)} %fusion.70), channel_id=1, source_target_pairs={{0,1},{1,0},{2,3},{3,2},{4,5},{5,4},{6,7},{7,6},{8,9},{9,8},{10,11... | collective-permute-start | bytes 3145736 | tf_op jit(solution)/shard_map/ppermute | solution.py:525
  281.4 31.3 %copy-start.9 = (bf16[512,1024]{1,0:T(8,128)(2,1)S(1)}, bf16[512,1024]{1,0:T(8,128)(2,1)}, u32[]{:S(2)}) copy-start(bf16[512,1024]{1,0:T(8,128)(2,1)} %refs_2_.1) | copy-start | bytes 3145732
  360.5 4.1 %copy-start.12 = (f32[512,1024]{1,0:T(8,128)S(1)}, f32[512,1024]{1,0:T(8,128)}, u32[]{:S(2)}) copy-start(f32[512,1024]{1,0:T(8,128)} %copy-done.10) | copy-start | bytes 6291460
  360.5 4.1 %copy-start.25 = (bf16[1024,2048]{1,0:T(8,128)(2,1)S(1)}, bf16[1024,2048]{1,0:T(8,128)(2,1)}, u32[]{:S(2)}) copy-start(bf16[1024,2048]{1,0:T(8,128)(2,1)} %all-gather.5.cloned.1.call-done) | copy-start | bytes 12582916
  (13 other events, 28.9 us)
Sparse Core Ops, SparseCore 0:
  10.2 58.0 all-gather.4
  70.5 52.0 all-gather.2
  169.1 75.7 reduce-scatter.2
  249.1 71.3 reduce-scatter.4

commit v4 on v3

--- a/solution.py
+++ b/solution.py
@@ -712,6 +712,9 @@
         .reshape((chips, 2, parts) + tile)
         .transpose(2, 1, 0, 3, 4)
     )
+    output, summed_down, packed_grads = lax.optimization_barrier(
+        (output.astype(BF16), summed_down.T, packed_grads)
+    )
     summed_first, sums = reduce_call(
         grad_first.reshape(chips, 2, -1, grad_first.shape[1]), packed_grads, chips, parts
     )
@@ -721,7 +724,7 @@
     )
     summed_qkv = jnp.stack([summed_first[:, n * width : (n + 1) * width] for n in range(3)])
     return (
-        output.astype(BF16),
+        output,
         grad_inputs.astype(BF16),
         sum_gain_a,
         sum_shift_a,
@@ -733,7 +736,7 @@
         sum_shift_b,
         summed_up,
         sums[at + n_qv : end].reshape(bias_up.shape),
-        summed_down.T,
+        summed_down,
         sum_down_shift,
     )
 

time: 386 us -> 383 us (level)
    unnamed x76 -> x82, local copies, waits for them, and re-layouts: 12.7 us -> 13.7 us
where the time goes in v4:
time: 383 us; the launch traced here: 377 us
  Pallas kernels  130 us (34%)
  waiting for transfers between devices  99.4 us (26%)
  matrix products  84.7 us (22%)
  local copies, waits for them, and re-layouts  23.3 us (6%)
  other arithmetic  21.8 us (6%)
  between operations  14.7 us (4%)
  starting transfers between devices  3.87 us (1%)
    ppermute x3, waiting for transfers between devices, scatter_rows(): lax.ppermute(product(blocks[1]).astype(BF16), 'tensor', [(0, 1), (1, 0)])  78.1 us
    pallas_call x1, Pallas kernels, gather_call(): pl.pallas_call(functools.partial(gather_kernel, chips, parts), out_shape=...  51.8 us
    pallas_call x2, Pallas kernels, attention_call(): pl.pallas_call(kernel, grid=(group // length, width // PAIR), out_shape=[...  40.4 us
    pallas_call x1, Pallas kernels, reduce_call(): pl.pallas_call(functools.partial(reduce_kernel, chips, parts), out_shape=...  37.3 us
    dot_general x8, matrix products, mm(): lax.dot_general(a, b, (((1,), (0,)), ((), ())), preferred_element_type=F32)  32.8 us
    dot_general x8, matrix products, mm_t(): lax.dot_general(a, b, (((1,), (1,)), ((), ())), preferred_element_type=F32)  31.6 us
    dot_general x4, matrix products, t_mm(): lax.dot_general(a, b, (((0,), (0,)), ((), ())), preferred_element_type=F32)  20.3 us
    ppermute x2, waiting for transfers between devices, gather_rows(): return [mine, lax.ppermute(mine, 'tensor', [(0, 1), (1, 0)])]  19.8 us
  transfers between devices with their start and end apart: 10, of which 5 were waited for; matrix products, arithmetic and copies ran while one was open for 26% of the time, Pallas kernels for 34%

profile of v4, /device:TPU:0, one launch (start us, length us, event | category | flops | bytes accessed | tf_op | source)
XLA Modules:
  0.0 377.3 jit_solution(3939877425667010577)
XLA Ops:
  14.3 51.8 %shard_map.245 = (bf16[8,2,64,2048]{3,2,1,0:T(8,128)(2,1)}, f32[2,8,2,8,128]{4,3,2,1,0:T(8,128)}, bf16[512,1024]{1,0:T(8,128)(2,1)}, bf16[512,1024]{1,0:T(8,128)(2,1)}) custom-call(bf16[64,2048]{1,0:T(8,128)(2,1)} %pad_maximum_fusion.6.refs_0_, f32[8,128]{1,0:T(8,128)} %pad_bitcast_fusion.1.refs_1_, bf16[512,1024]{1,0:T(8,128)(2,1)} %refs_2_.1, ...), custom_call_target="tpu_custom_call" | custom-call | bytes 8388608 | tf_op jit(solution)/shard_map/pallas_call | solution.py:315
  70.5 2.1 copy-done.30
  76.6 14.6 %shard_map.246 = bf16[1024,512]{1,0:T(8,128)(2,1)S(1)} custom-call(s32[1]{0:T(128)} %bitcast.flip_ref, f32[8]{0:T(128)S(1)} %multiply_exponential_fusion.slope_ref, bf16[1024,512]{1,0:T(8,128)(2,1)S(1)} %get-tuple-element.103.q_ref, bf16[1024,512]{1,0:T(8,128)(2,1)S(1)} %get-tuple-element.104.k_ref, bf16[1024,512]{1,0:T(8,128)(2,1)S(1)} %get-tuple-element.102.v_ref), custom_call_target="tpu_custom_call" | custom-call | flops 4294967296 | bytes 4194304 | tf_op jit(solution)/shard_map/pallas_call | solution.py:159
  94.3 25.0 %collective-permute-done = bf16[512,1024]{1,0:T(8,128)(2,1)} collective-permute-done((bf16[512,1024]{1,0:T(8,128)(2,1)}, bf16[512,1024]{1,0:T(8,128)(2,1)}, u32[]{:S(2)}, u32[]{:S(2)}) %collective-permute-start) | collective-permute-done | bytes 1048608 | tf_op jit(solution)/shard_map/ppermute | solution.py:525
  119.2 2.5 fusion.98
  123.7 6.5 %fusion.100 = f32[512,2048]{1,0:T(8,128)} fusion(bf16[512,1024]{1,0:T(8,128)(2,1)S(1)} %copy-done.16, bf16[1024,2048]{1,0:T(8,128)(2,1)} %all-gather.5.cloned.1.call-done), kind=kOutput, calls=%fused_computation.165 | convolution fusion | flops 2147483648 | bytes 9437184 | tf_op jit(solution)/shard_map/dot_general | solution.py:43
  130.2 4.7 %fusion.99 = f32[512,2048]{1,0:T(8,128)S(1)} fusion(bf16[512,1024]{1,0:T(8,128)(2,1)S(1)} %add_convert_fusion.1, bf16[1024,2048]{1,0:T(8,128)(2,1)} %all-gather.3.cloned.1.call-done), kind=kOutput, calls=%fused_computation.164 | convolution fusion | flops 2147483648 | bytes 9437184 | tf_op jit(solution)/shard_map/dot_general | solution.py:43
  135.0 2.4 fusion.101
  137.4 11.0 %collective-permute-done.1 = bf16[512,1024]{1,0:T(8,128)(2,1)} collective-permute-done((bf16[512,1024]{1,0:T(8,128)(2,1)S(1)}, bf16[512,1024]{1,0:T(8,128)(2,1)}, u32[]{:S(2)}, u32[]{:S(2)}) %collective-permute-start.1) | collective-permute-done | bytes 1048608 | tf_op jit(solution)/shard_map/ppermute | solution.py:520
  148.4 11.3 %multiply_convert_fusion = (bf16[512,2048]{1,0:T(8,128)(2,1)S(1)}, bf16[512,2048]{1,0:T(8,128)(2,1)}, bf16[512,2048]{1,0:T(8,128)(2,1)}, bf16[512,2048]{1,0:T(8,128)(2,1)S(1)}) fusion(f32[2048]{0:T(1024)S(1)} %add.185, f32[512,2048]{1,0:T(8,128)S(1)} %fusion.101, f32[512,2048]{1,0:T(8,128)S(1)} %copy-done.34, f32[512,2048]{1,0:T(8,128)S(1)} %fusion.99, ...), kind=kOutput, calls=%fused_computation.25 | convolution fusion | flops 2195718144 | bytes 26222592 | tf_op jit(solution)/shard_map/dot_general | solution.py:43
  161.7 6.3 %fusion.18 = bf16[1024,2048]{1,0:T(8,128)(2,1)} fusion(bf16[512,2048]{1,0:T(8,128)(2,1)S(1)} %get-tuple-element.35, bf16[512,2048]{1,0:T(8,128)(2,1)S(1)} %get-tuple-element.34, bf16[512,1024]{1,0:T(8,128)(2,1)S(1)} %copy-done.33, bf16[512,1024]{1,0:T(8,128)(2,1)S(1)} %copy-done.16), kind=kOutput, calls=%fused_computation.27 | convolution fusion | flops 4309647360 | bytes 10485760 | tf_op jit(solution)/shard_map/dot_general | solution.py:51
  168.1 6.3 %convolution_convert_fusion.4 = bf16[512,1024]{1,0:T(8,128)(2,1)} fusion(bf16[512,2048]{1,0:T(8,128)(2,1)} %get-tuple-element.99, bf16[1024,2048]{1,0:T(8,128)(2,1)} %all-gather.3.cloned.1.call-done), kind=kOutput, calls=%fused_computation.104 | convolution fusion | flops 2148007936 | bytes 7340032 | tf_op jit(solution)/shard_map/dot_general | solution.py:47
  174.9 24.2 %collective-permute-done.2 = bf16[512,1024]{1,0:T(8,128)(2,1)} collective-permute-done((bf16[512,1024]{1,0:T(8,128)(2,1)}, bf16[512,1024]{1,0:T(8,128)(2,1)}, u32[]{:S(2)}, u32[]{:S(2)}) %collective-permute-start.2) | collective-permute-done | bytes 1048608 | tf_op jit(solution)/shard_map/ppermute | solution.py:525
  199.0 6.7 %multiply_reduce_fusion = (f32[1024]{0:T(1024)S(1)}, f32[512]{0:T(512)S(1)}, f32[512]{0:T(512)S(1)}, f32[1024]{0:T(1024)S(1)}, f32[512,1024]{1,0:T(8,128)S(1)}) fusion(f32[512,1024]{1,0:T(8,128)S(1)} %copy-done.11, f32[512]{0:T(512)S(1)} %add_rsqrt_fusion, f32[512]{0:T(512)S(1)} %broadcast_multiply_fusion.4, bf16[512,1024]{1,0:T(8,128)(2,1)} %collective-permute-done.2, ...), kind=kOutput, calls=%fused_computation.82 | convolution fusion | flops 2153247744 | bytes 11554816 | tf_op jit(solution)/shard_map/dot_general | solution.py:47
  205.7 2.5 fusion.94
  211.3 7.5 %convolution_convert_fusion.1 = bf16[1024,2048]{1,0:T(8,128)(2,1)} fusion(bf16[512,2048]{1,0:T(8,128)(2,1)S(1)} %copy-done.17, bf16[512,2048]{1,0:T(8,128)(2,1)S(1)} %copy-done.18, bf16[512,1024]{1,0:T(8,128)(2,1)} %collective-permute-done.1, bf16[512,1024]{1,0:T(8,128)(2,1)S(1)} %copy-done.22), kind=kOutput, calls=%fused_computation.29 | convolution fusion | flops 4309647360 | bytes 10485760 | tf_op jit(solution)/shard_map/dot_general | solution.py:51
  218.7 2.4 convert_reduce_fusion
  221.8 2.1 convolution_convert_fusion.6
  223.9 8.8 %collective-permute-done.3 = bf16[512,1024]{1,0:T(8,128)(2,1)} collective-permute-done((bf16[512,1024]{1,0:T(8,128)(2,1)S(1)}, bf16[512,1024]{1,0:T(8,128)(2,1)}, u32[]{:S(2)}, u32[]{:S(2)}) %collective-permute-start.3) | collective-permute-done | bytes 1048608 | tf_op jit(solution)/shard_map/ppermute | solution.py:520
  232.7 2.2 convolution_convert_fusion.5
  236.0 3.4 convolution_convert_fusion.3
  239.4 25.8 %shard_map.247 = (bf16[1024,512]{1,0:T(8,128)(2,1)S(1)}, bf16[1024,512]{1,0:T(8,128)(2,1)S(1)}, bf16[1024,512]{1,0:T(8,128)(2,1)S(1)}) custom-call(s32[1]{0:T(128)} %bitcast.flip_ref, f32[8]{0:T(128)S(1)} %multiply_exponential_fusion.slope_ref, bf16[1024,512]{1,0:T(8,128)(2,1)S(1)} %copy-done.3, bf16[1024,512]{1,0:T(8,128)(2,1)S(1)} %copy-done.5, ...), custom_call_target="tpu_custom_call" | custom-call | flops 10737418240 | bytes 7340032 | tf_op jit(solution)/shard_map/pallas_call | solution.py:159
  266.8 2.1 copy-done.31
  272.6 2.7 fusion.75
  275.3 3.9 %convolution_convert_fusion = bf16[1024,1536]{1,0:T(8,128)(2,1)S(1)} fusion(bf16[1024,1536]{1,0:T(8,128)(2,1)S(1)} %constant_dynamic-update-slice_fusion, bf16[512,1024]{1,0:T(8,128)(2,1)S(1)} %copy-done.24, bf16[512,1024]{1,0:T(8,128)(2,1)S(1)} %copy-done.26), kind=kOutput, calls=%fused_computation.28 | convolution fusion | flops 3226992640 | bytes 8388608 | tf_op jit(solution)/shard_map/dot_general | solution.py:51
  279.2 2.6 pad_maximum_fusion.1
  281.9 29.0 %collective-permute-done.5 = bf16[512,1024]{1,0:T(8,128)(2,1)S(1)} collective-permute-done((bf16[512,1024]{1,0:T(8,128)(2,1)S(1)}, bf16[512,1024]{1,0:T(8,128)(2,1)S(1)}, u32[]{:S(2)}, u32[]{:S(2)}) %collective-permute-start.5) | collective-permute-done | bytes 1048608 | tf_op jit(solution)/shard_map/ppermute | solution.py:525
  310.9 3.7 fusion.34
  314.9 3.5 fusion.38
  318.4 5.4 %add_convert_fusion = bf16[512,1024]{1,0:T(8,128)(2,1)} fusion(f32[512,1024]{1,0:T(8,128)S(1)} %copy-done.12, bf16[512,1024]{1,0:T(8,128)(2,1)} %collective-permute-done.4, bf16[512,2048]{1,0:T(8,128)(2,1)} %copy-done.35, bf16[1024,2048]{1,0:T(8,128)(2,1)S(1)} %copy-done.29, f32[1024]{0:T(1024)S(1)} %add.197), kind=kOutput, calls=%fused_computation.84 | convolution fusion | flops 2150105088 | bytes 10489856 | tf_op jit(solution)/shard_map/dot_general | solution.py:47
  325.6 2.2 copy-done
  327.8 37.3 %shard_map.248 = (f32[64,2048]{1,0:T(8,128)S(1)}, f32[8,128]{1,0:T(8,128)S(1)}) custom-call(bf16[8,2,64,2048]{3,2,1,0:T(8,128)(2,1)S(1)} %bitcast.77, f32[2,2,8,8,128]{4,3,2,1,0:T(8,128)S(1)} %bitcast.78), custom_call_target="tpu_custom_call" | custom-call | bytes 8388608 | tf_op jit(solution)/shard_map/pallas_call | solution.py:459
  (190 shorter events, 40.2 us)
Async XLA Ops:
  7.2 116.3 %all-gather.5.cloned.1.call-start = ((), (), s32[]{:S(2)}) async-start(), calls=%async_computation.3 | async-start | bytes 4456448 | tf_op jit(solution)/shard_map/all_gather | solution.py:513
  7.9 122.3 %all-gather.3.cloned.1.call-start = ((), (), s32[]{:S(2)}) async-start(), calls=%async_computation.2 | async-start | bytes 4456448 | tf_op jit(solution)/shard_map/all_gather | solution.py:513
  8.7 315.2 %reduce-scatter.3.cloned.1.call-start = ((), (), s32[]{:S(2)}) async-start(), calls=%async_computation.4 | async-start | bytes 4456448 | tf_op jit(solution)/shard_map/reduce_scatter | solution.py:516
  14.3 54.1 %copy-start.8 = (bf16[512,1024]{1,0:T(8,128)(2,1)S(1)}, bf16[512,1024]{1,0:T(8,128)(2,1)}, u32[]{:S(2)}) copy-start(bf16[512,1024]{1,0:T(8,128)(2,1)} %refs_2_.1) | copy-start | bytes 3145732
  70.5 3.9 %copy-start.23 = (bf16[512,1024]{1,0:T(8,128)(2,1)}, bf16[512,1024]{1,0:T(8,128)(2,1)S(1)}, u32[]{:S(2)}) copy-start(bf16[512,1024]{1,0:T(8,128)(2,1)S(1)} %get-tuple-element.123) | copy-start | bytes 3145732
  70.5 3.9 %copy-start.25 = (bf16[512,1024]{1,0:T(8,128)(2,1)}, bf16[512,1024]{1,0:T(8,128)(2,1)S(1)}, u32[]{:S(2)}) copy-start(bf16[512,1024]{1,0:T(8,128)(2,1)S(1)} %get-tuple-element.124) | copy-start | bytes 3145732
  76.5 14.6 %copy-start.1 = (bf16[1024,512]{1,0:T(8,128)(2,1)}, bf16[1024,512]{1,0:T(8,128)(2,1)S(1)}, u32[]{:S(2)}) copy-start(bf16[1024,512]{1,0:T(8,128)(2,1)S(1)} %get-tuple-element.102.v_ref) | copy-start | bytes 3145732
  76.6 14.6 %copy-start.2 = (bf16[1024,512]{1,0:T(8,128)(2,1)}, bf16[1024,512]{1,0:T(8,128)(2,1)S(1)}, u32[]{:S(2)}) copy-start(bf16[1024,512]{1,0:T(8,128)(2,1)S(1)} %get-tuple-element.103.q_ref) | copy-start | bytes 3145732
  76.6 14.6 %copy-start.4 = (bf16[1024,512]{1,0:T(8,128)(2,1)}, bf16[1024,512]{1,0:T(8,128)(2,1)S(1)}, u32[]{:S(2)}) copy-start(bf16[1024,512]{1,0:T(8,128)(2,1)S(1)} %get-tuple-element.104.k_ref) | copy-start | bytes 3145732
  91.2 30.6 %copy-start.6 = (bf16[1024,512]{1,0:T(8,128)(2,1)}, bf16[1024,512]{1,0:T(8,128)(2,1)S(1)}, u32[]{:S(2)}) copy-start(bf16[1024,512]{1,0:T(8,128)(2,1)S(1)} %shard_map.246) | copy-start | bytes 3145732
  92.9 26.3 %collective-permute-start = (bf16[512,1024]{1,0:T(8,128)(2,1)}, bf16[512,1024]{1,0:T(8,128)(2,1)}, u32[]{:S(2)}, u32[]{:S(2)}) collective-permute-start(bf16[512,1024]{1,0:T(8,128)(2,1)} %convolution_convert_fusion.2), channel_id=1, source_target_pairs={{0,1},{1,0},{2,3},{3,2},{4,5},{5,4},{6,7},{7,6},{8,9},{9,8},{10,11... | collective-permute-start | bytes 3145736 | tf_op jit(solution)/shard_map/ppermute | solution.py:525
  123.1 7.1 %copy-start.21 = (bf16[512,1024]{1,0:T(8,128)(2,1)}, bf16[512,1024]{1,0:T(8,128)(2,1)S(1)}, u32[]{:S(2)}) copy-start(bf16[512,1024]{1,0:T(8,128)(2,1)S(1)} %add_convert_fusion.1) | copy-start | bytes 3145732
  123.1 25.3 %collective-permute-start.1 = (bf16[512,1024]{1,0:T(8,128)(2,1)S(1)}, bf16[512,1024]{1,0:T(8,128)(2,1)}, u32[]{:S(2)}, u32[]{:S(2)}) collective-permute-start(bf16[512,1024]{1,0:T(8,128)(2,1)S(1)} %add_convert_fusion.1), channel_id=1, source_target_pairs={{0,1},{1,0},{2,3},{3,2},{4,5},{5,4},{6,7},{7,6},{8,9},{9,8},{10,11... | collective-permute-start | bytes 3145736 | tf_op jit(solution)/shard_map/ppermute | solution.py:520
  130.2 4.7 %copy-start.33 = (bf16[512,1024]{1,0:T(8,128)(2,1)S(1)}, bf16[512,1024]{1,0:T(8,128)(2,1)}, u32[]{:S(2)}) copy-start(bf16[512,1024]{1,0:T(8,128)(2,1)} %get-tuple-element.33) | copy-start | bytes 3145732
  130.2 4.7 %copy-start.27 = (bf16[1024,2048]{1,0:T(8,128)(2,1)S(1)}, bf16[1024,2048]{1,0:T(8,128)(2,1)}, u32[]{:S(2)}) copy-start(bf16[1024,2048]{1,0:T(8,128)(2,1)} %all-gather.5.cloned.1.call-done) | copy-start | bytes 12582916
  135.0 13.4 %copy-start.32 = (bf16[1024,2048]{1,0:T(8,128)(2,1)S(1)}, bf16[1024,2048]{1,0:T(8,128)(2,1)}, u32[]{:S(2)}) copy-start(bf16[1024,2048]{1,0:T(8,128)(2,1)} %all-gather.3.cloned.1.call-done) | copy-start | bytes 12582916
  135.0 13.4 %copy-start.34 = (f32[512,2048]{1,0:T(8,128)S(1)}, f32[512,2048]{1,0:T(8,128)}, u32[]{:S(2)}) copy-start(f32[512,2048]{1,0:T(8,128)} %fusion.100) | copy-start | bytes 12582916
  168.0 200.7 %reduce-scatter.5.cloned.1.call-start = ((), (), s32[]{:S(2)}) async-start(), calls=%async_computation.5 | async-start | bytes 4456448 | tf_op jit(solution)/shard_map/reduce_scatter | solution.py:516
  168.1 30.9 %copy-start.11 = (f32[512,1024]{1,0:T(8,128)S(1)}, f32[512,1024]{1,0:T(8,128)}, u32[]{:S(2)}) copy-start(f32[512,1024]{1,0:T(8,128)} %copy-done.10) | copy-start | bytes 6291460
  174.4 24.6 %collective-permute-start.2 = (bf16[512,1024]{1,0:T(8,128)(2,1)}, bf16[512,1024]{1,0:T(8,128)(2,1)}, u32[]{:S(2)}, u32[]{:S(2)}) collective-permute-start(bf16[512,1024]{1,0:T(8,128)(2,1)} %convolution_convert_fusion.4), channel_id=1, source_target_pairs={{0,1},{1,0},{2,3},{3,2},{4,5},{5,4},{6,7},{7,6},{8,9},{9,8},{10,11... | collective-permute-start | bytes 3145736 | tf_op jit(solution)/shard_map/ppermute | solution.py:525
  205.7 4.1 %copy-start.18 = (bf16[512,2048]{1,0:T(8,128)(2,1)S(1)}, bf16[512,2048]{1,0:T(8,128)(2,1)}, u32[]{:S(2)}) copy-start(bf16[512,2048]{1,0:T(8,128)(2,1)} %get-tuple-element.121) | copy-start | bytes 6291460
  209.7 12.1 %copy-start.19 = (bf16[512,1024]{1,0:T(8,128)(2,1)}, bf16[512,1024]{1,0:T(8,128)(2,1)S(1)}, u32[]{:S(2)}) copy-start(bf16[512,1024]{1,0:T(8,128)(2,1)S(1)} %convert_element_type.126) | copy-start | bytes 3145732
  209.7 23.0 %collective-permute-start.3 = (bf16[512,1024]{1,0:T(8,128)(2,1)S(1)}, bf16[512,1024]{1,0:T(8,128)(2,1)}, u32[]{:S(2)}, u32[]{:S(2)}) collective-permute-start(bf16[512,1024]{1,0:T(8,128)(2,1)S(1)} %convert_element_type.126), channel_id=1, source_target_pairs={{0,1},{1,0},{2,3},{3,2},{4,5},{5,4},{6,7},{7,6},{8,9},{9,8},{10,11... | collective-permute-start | bytes 3145736 | tf_op jit(solution)/shard_map/ppermute | solution.py:520
  221.8 14.2 %copy-start.37 = (bf16[512,2048]{1,0:T(8,128)(2,1)S(1)}, bf16[512,2048]{1,0:T(8,128)(2,1)}, u32[]{:S(2)}) copy-start(bf16[512,2048]{1,0:T(8,128)(2,1)} %copy-done.36) | copy-start | bytes 6291460
  223.9 12.1 %copy-start.28 = (bf16[1024,2048]{1,0:T(8,128)(2,1)S(1)}, bf16[1024,2048]{1,0:T(8,128)(2,1)}, u32[]{:S(2)}) copy-start(bf16[1024,2048]{1,0:T(8,128)(2,1)} %all-gather.5.cloned.1.call-done) | copy-start | bytes 12582916
  266.2 52.2 %collective-permute-start.4 = (bf16[512,1024]{1,0:T(8,128)(2,1)}, bf16[512,1024]{1,0:T(8,128)(2,1)}, u32[]{:S(2)}, u32[]{:S(2)}) collective-permute-start(bf16[512,1024]{1,0:T(8,128)(2,1)} %convolution_convert_fusion.3), channel_id=1, source_target_pairs={{0,1},{1,0},{2,3},{3,2},{4,5},{5,4},{6,7},{7,6},{8,9},{9,8},{10,11... | collective-permute-start | bytes 3145736 | tf_op jit(solution)/shard_map/ppermute | solution.py:648
  268.9 3.7 copy-start.7
  268.9 3.7 copy-start.20
  270.7 40.1 %collective-permute-start.5 = (bf16[512,1024]{1,0:T(8,128)(2,1)S(1)}, bf16[512,1024]{1,0:T(8,128)(2,1)S(1)}, u32[]{:S(2)}, u32[]{:S(2)}) collective-permute-start(bf16[512,1024]{1,0:T(8,128)(2,1)S(1)} %fusion.70), channel_id=1, source_target_pairs={{0,1},{1,0},{2,3},{3,2},{4,5},{5,4},{6,7},{7,6},{8,9},{9,8},{10,11... | collective-permute-start | bytes 3145736 | tf_op jit(solution)/shard_map/ppermute | solution.py:525
  279.2 31.6 %copy-start.9 = (bf16[512,1024]{1,0:T(8,128)(2,1)S(1)}, bf16[512,1024]{1,0:T(8,128)(2,1)}, u32[]{:S(2)}) copy-start(bf16[512,1024]{1,0:T(8,128)(2,1)} %refs_2_.1) | copy-start | bytes 3145732
  310.9 4.0 %copy-start.14 = (f32[512,1024]{1,0:T(8,128)S(1)}, f32[512,1024]{1,0:T(8,128)}, u32[]{:S(2)}) copy-start(f32[512,1024]{1,0:T(8,128)} %copy-done.13) | copy-start | bytes 6291460
  314.9 3.5 copy-start.12
  (16 other events, 38.5 us)
Sparse Core Ops, SparseCore 0:
  10.2 58.0 all-gather.4
  70.5 51.8 all-gather.2
  168.2 75.6 reduce-scatter.2
  248.1 71.3 reduce-scatter.4
